TPU v7x, 256 devices: a whole 4x4x8 slice. The times are simulated.
256 devices in a mesh: seq: 32 (over y, z_lo, core), head: 8 (over x, z_hi).
Axes of the slice: x: 4, y: 4, z: 8 (z_hi: 2, z_lo: 4; z = z_hi * 4 + z_lo), core: 2. Of those that a mesh axis runs over, the one named last changes fastest.
Arguments:
- latent_queries: bfloat16 [4096, 128, 576], P('seq', 'head'), may hold values from -16 to 16
- latent_keys: bfloat16 [2048, 576], P('seq'), may hold values from -6 to 6
- index_queries: bfloat16 [4096, 64, 128], P('seq', 'head'), may hold values from -8 to 8
- index_keys: bfloat16 [2048, 128], P('seq'), may hold values from -6 to 6
- head_weights: float32 [4096, 64], P('seq', 'head'), may hold values from -18 to 18
- visible: int32 [4096], P('seq'), may hold values from 1 to 2048, as said below
Outputs:
- grad_index_queries: bfloat16 [4096, 64, 128], P('seq', 'head')
- grad_head_weights: float32 [4096, 64], P('seq', 'head')
- grad_index_keys: float32 [2048, 128], P('seq')
Inputs may be any that keep to these rules, and one draw needn't show every extreme that they name: Row t sees keys 0 to visible[t] - 1, never more than (t * 2048) // 4096 + 1 of them; the last row sees all 2048 keys.
All inputs are finite; a program needn't handle non-finite values.
Results may differ from a plain program's by a relative error of at most 0.0049.
Values may be sent and summed in bfloat16 or wider, within the bound.
No kernel may reach another device: no remote copies, remote signals or barrier semaphores. Data moves between devices by JAX's collectives and lax.ppermute only.
A program may use at most 64 MiB of HBM per device.

v0:
```python
import jax
import jax.numpy as jnp
from jax import lax
from jax.sharding import PartitionSpec as P

MLA_HEADS = 128
INDEX_HEADS = 64


mla_scale = 192.0 ** (-0.5)
loss_weight = 16.0
neg_fill = -1e30
start_peak = -5e29


def latent_scores(queries, portion, visible):
    row_count, head_count, width = queries.shape
    flat = queries.reshape(row_count * head_count, width)
    scores = (
        lax.dot_general(portion, flat, (((1,), (1,)), ((), ())), preferred_element_type=jnp.float32)
        * mla_scale
    )
    key_ids = lax.broadcasted_iota(jnp.int32, (portion.shape[0], 1), 0)
    limit = jnp.broadcast_to(visible[:, None], (row_count, head_count)).reshape(
        1, row_count * head_count
    )
    return jnp.where(key_ids < limit, scores, neg_fill)


def stats_update(status, queries, portion, visible):
    maxima, totals = status
    row_count, head_count = maxima.shape
    scores = latent_scores(queries, portion, visible)
    old_max = maxima.reshape(row_count * head_count)
    new_max = jnp.maximum(old_max, jnp.max(scores, axis=0))
    new_total = jnp.sum(jnp.exp(scores - new_max[None, :]), axis=0)
    return (new_max.reshape(row_count, head_count), new_total.reshape(row_count, head_count))


def target_update(queries, portion, visible, normalizer):
    row_count, head_count = normalizer.shape
    key_count = portion.shape[0]
    scores = latent_scores(queries, portion, visible)
    probs = jnp.exp(scores - normalizer.reshape(1, row_count * head_count))
    summed = jnp.sum(probs.reshape(key_count, row_count, head_count), axis=2)
    return summed.T / MLA_HEADS


def index_logits(index_queries, index_all, head_weights, span):
    row_count = index_queries.shape[0]
    key_count = index_all.shape[0]
    dot_scale = index_queries.shape[2] ** (-0.5)
    head_scale = INDEX_HEADS ** (-0.5)

    def one_span(number, logits):
        offset = number * span
        portion = lax.dynamic_slice_in_dim(index_all, offset, span, 0)
        products = (
            jnp.einsum("thd,kd->thk", index_queries, portion, preferred_element_type=jnp.float32)
            * dot_scale
        )
        summed = jnp.sum(head_weights[:, :, None] * jnp.maximum(products, 0.0), axis=1) * head_scale
        return lax.dynamic_update_slice_in_dim(logits, summed, offset, 1)

    return lax.fori_loop(
        0, key_count // span, one_span, jnp.zeros((row_count, key_count), jnp.float32)
    )


def index_backward(index_queries, index_all, head_weights, row_grad, span):
    row_count, head_count, depth = index_queries.shape
    key_count = index_all.shape[0]
    dot_scale = depth ** (-0.5)
    head_scale = INDEX_HEADS ** (-0.5)
    weighted = head_weights * head_scale

    def one_span(number, running):
        query_grad, weight_grad, key_grad = running
        offset = number * span
        portion = lax.dynamic_slice_in_dim(index_all, offset, span, 0)
        slope = lax.dynamic_slice_in_dim(row_grad, offset, span, 1)
        products = (
            jnp.einsum("thd,kd->thk", index_queries, portion, preferred_element_type=jnp.float32)
            * dot_scale
        )
        edge_grad = jnp.where(products > 0.0, slope[:, None, :] * weighted[:, :, None], 0.0).astype(
            jnp.bfloat16
        )
        query_grad = query_grad + jnp.einsum(
            "thk,kd->thd", edge_grad, portion, preferred_element_type=jnp.float32
        )
        weight_grad = weight_grad + jnp.sum(slope[:, None, :] * jnp.maximum(products, 0.0), axis=2)
        key_term = jnp.einsum(
            "thk,thd->kd", edge_grad, index_queries, preferred_element_type=jnp.float32
        )
        key_grad = lax.dynamic_update_slice_in_dim(key_grad, key_term, offset, 0)
        return (query_grad, weight_grad, key_grad)

    initial = (
        jnp.zeros((row_count, head_count, depth), jnp.float32),
        jnp.zeros((row_count, head_count), jnp.float32),
        jnp.zeros((key_count, depth), jnp.float32),
    )
    query_grad, weight_grad, key_grad = lax.fori_loop(0, key_count // span, one_span, initial)
    return (
        (query_grad * dot_scale).astype(jnp.bfloat16),
        weight_grad * head_scale,
        key_grad * dot_scale,
    )


def body(latent_queries, latent_keys, index_queries, index_keys, head_weights, visible):
    row_count = latent_queries.shape[0]
    head_count = latent_queries.shape[1]
    key_count = latent_keys.shape[0] * lax.axis_size("seq")
    span = min(512, key_count)
    initial = (
        jnp.full((row_count, head_count), start_peak, jnp.float32),
        jnp.zeros((row_count, head_count), jnp.float32),
    )
    status = initial
    status = stats_update(
        status, latent_queries, lax.all_gather(latent_keys, "seq", axis=0, tiled=True), visible
    )
    collected = lax.all_gather(index_keys, "seq", axis=0, tiled=True)
    status, index_all = (status, collected)
    normalizer = status[0] + jnp.log(status[1])
    logit_part = index_logits(index_queries, index_all, head_weights, span)
    target_part = target_update(
        latent_queries, lax.all_gather(latent_keys, "seq", axis=0, tiled=True), visible, normalizer
    )
    target, logits = lax.psum((target_part, logit_part), "head")
    columns = lax.broadcasted_iota(jnp.int32, (1, key_count), 1)
    logits = jnp.where(columns < visible[:, None], logits, neg_fill)
    row_peak = jnp.max(logits, axis=1, keepdims=True)
    weights = jnp.exp(logits - row_peak)
    index_prob = weights / jnp.sum(weights, axis=1, keepdims=True)
    row_grad = loss_weight * (index_prob - target)
    query_grad, weight_grad, key_term = index_backward(
        index_queries, index_all, head_weights, row_grad, span
    )
    owned = lax.psum_scatter(key_term, "seq", scatter_dimension=0, tiled=True)
    key_grad = lax.psum(owned, "head")
    return (query_grad, weight_grad, key_grad)


def solution(mesh):
    placed = (
        P("seq", "head", None),
        P("seq", None),
        P("seq", "head", None),
        P("seq", None),
        P("seq", "head"),
        P("seq"),
    )
    return jax.shard_map(
        body,
        mesh=mesh,
        in_specs=placed,
        out_specs=(P("seq", "head", None), P("seq", "head"), P("seq", None)),
        check_vma=False,
    )
```

profile of v0, /device:TPU:0, one launch (start us, length us, event | category | flops | bytes accessed | tf_op | source)
XLA Modules:
  0.0 520.9 jit_solution(5947452064144899481)
XLA Ops:
  8.8 4.9 copy.23
  13.8 48.6 %all_gather.7 = bf16[2048,128]{1,0:T(8,128)(2,1)} all-gather(bf16[64,128]{1,0:T(8,128)(2,1)S(1)} %copy-done.4), channel_id=1, replica_groups=mesh['seq'=32,'head'=8] {'seq'}, dimensions={0}, use_global_device_ids=true | all-gather | bytes 540672 | tf_op jit(solution)/shard_map/all_gather | solution.py:125
  62.5 6.4 %while.31 = (s32[]{:T(128)}, f32[128,2048]{1,0:T(8,128)S(1)}, f32[128,8]{0,1:T(8,128)S(1)}, bf16[2048,128]{1,0:T(8,128)(2,1)}, bf16[128,8,128]{2,0,1:T(8,128)(2,...) while((s32[]{:T(128)}, f32[128,2048]{1,0:T(8,128)S(1)}, f32[128,8]{0,1:T(8,128)S(1)}, ...), condition=%wide.region_2.3_spmd, body=%wide.region_0.0_spmd.sunk | while | flops 136314880 | bytes 2232467 | solution.py:65
  62.5 1.4 multiply_reduce_fusion.2
  64.1 1.4 multiply_reduce_fusion.2
  65.7 1.4 multiply_reduce_fusion.2
  67.3 1.4 multiply_reduce_fusion.2
  68.9 3.6 all-gather.2.cloned.1.call-done
  72.5 10.9 %fusion.12 = (f32[2048]{0:T(1024)S(1)}, f32[2048,2048]{0,1:T(8,128)S(1)}) fusion(s32[2048]{0:T(1024)S(1)} %lt.66, bf16[2048,576]{1,0:T(8,128)(2,1)} %all-gather.2.cloned.1.call-done, bf16[2048,576]{1,0:T(8,128)(2,1)} %bitcast.56), kind=kOutput, calls=%fused_computation.26 | convolution fusion | flops 4848613376 | bytes 21512192 | tf_op jit(solution)/shard_map/dot_general | solution.py:20
  83.4 5.6 %exponential_reduce_fusion = f32[2048]{0:T(1024)S(1)} fusion(f32[2048,2048]{0,1:T(8,128)S(1)} %get-tuple-element.339, f32[2048]{0:T(1024)S(1)} %broadcast_maximum_fusion, s32[2048]{0:T(1024)S(1)} %lt.66), kind=kLoop, calls=%fused_computation.23 | loop fusion | flops 20969472 | bytes 16801792 | tf_op jit(solution)/shard_map/reduce_sum | solution.py:36
  89.0 6.6 %bitcast_reduce_fusion = f32[2048,128]{0,1:T(8,128)S(1)} fusion(f32[2048,2048]{0,1:T(8,128)S(1)} %get-tuple-element.339, f32[2048]{0:T(1024)S(1)} %log_add_fusion, s32[2048]{0:T(1024)S(1)} %lt.66), kind=kLoop, calls=%fused_computation.21 | loop fusion | flops 20709376 | bytes 17842176 | tf_op jit(solution)/shard_map/reduce_sum | solution.py:45
  97.0 193.8 %all-reduce.3.cloned.1.call-done = (f32[128,2048]{1,0:T(8,128)}, f32[128,2048]{1,0:T(8,128)}) async-done(((f32[128,2048]{1,0:T(8,128)}, f32[128,2048]{1,0:T(8,128)}), (f32[128,2048]{1,0:T(8,128)}, f32[128,2048]{1,0:T(8,128)})) %all-reduce.3.cloned.1.call-update) | async-done | bytes 2097168 | tf_op jit(solution)/shard_map/psum | solution.py:132
  290.8 1.7 fusion.14
  292.5 1.6 fusion.15
  294.1 1.4 subtract_multiply_fusion
  296.6 20.9 %while.32 = (s32[]{:T(128)}, f32[128,8,128]{2,0,1:T(8,128)S(1)}, f32[128,8]{0,1:T(8,128)S(1)}, f32[2048,128]{1,0:T(8,128)}, bf16[2048,128]{1,0:T(8,128)(2,1)}, /...) while((s32[]{:T(128)}, f32[128,8,128]{2,0,1:T(8,128)S(1)}, ...), condition=%wide.region_12.13_spmd.clone, body=%wide.region_10.12_spmd.clone.sunk | while | flops 410256384 | bytes 10248382 | solution.py:104
  300.3 1.5 convolution_add_fusion.2
  305.5 1.5 convolution_add_fusion.2
  310.7 1.5 convolution_add_fusion.2
  313.4 1.4 fusion.34
  315.9 1.5 convolution_add_fusion.2
  317.5 2.3 broadcast_multiply_fusion
  321.5 140.3 %reduce-scatter.2.cloned.1.call-done = f32[64,128]{1,0:T(8,128)} async-done(((f32[2048,128]{1,0:T(8,128)}), f32[64,128]{1,0:T(8,128)}) %reduce-scatter.2.cloned.1.call-update) | async-done | bytes 32784 | tf_op jit(solution)/shard_map/reduce_scatter | solution.py:142
  461.8 52.7 %psum.23 = f32[64,128]{1,0:T(8,128)} all-reduce(f32[64,128]{1,0:T(8,128)} %reduce-scatter.2.cloned.1.call-done), channel_id=1, replica_groups=mesh['seq'=32,'head'=8] {'head'}, use_global_device_ids=true, to_apply=%region_14.15 | all-reduce | flops 8192 | bytes 65536 | tf_op jit(solution)/shard_map/psum | solution.py:143
  (64 shorter events, 19.7 us)
Async XLA Ops:
  7.2 6.5 %copy-start.3 = (bf16[128,8,128]{2,1,0:T(8,128)(2,1)S(1)}, bf16[128,8,128]{2,1,0:T(8,128)(2,1)}, u32[]{:S(2)}) copy-start(bf16[128,8,128]{2,1,0:T(8,128)(2,1)} %param.12) | copy-start | bytes 786436
  7.2 65.3 %all-gather.2.cloned.1.call-start = ((), (), s32[]{:S(2)}) async-start(), calls=%async_computation.1 | async-start | bytes 2703360 | tf_op jit(solution)/shard_map/all_gather | solution.py:130
  7.9 282.9 %all-reduce.3.cloned.1.call-start = ((), (), s32[]{:S(2)}) async-start(), calls=%async_computation.3 | async-start | bytes 4194304 | tf_op jit(solution)/shard_map/psum | solution.py:132
  8.8 5.0 copy-start.4
  8.8 53.7 %copy-start.6 = (f32[128,8]{0,1:T(8,128)S(1)}, f32[128,8]{0,1:T(8,128)}, u32[]{:S(2)}) copy-start(f32[128,8]{0,1:T(8,128)} %param.14) | copy-start | bytes 12292
  68.8 14.6 %copy-start.1 = (f32[128,2048]{1,0:T(8,128)}, f32[128,2048]{1,0:T(8,128)S(1)}, u32[]{:S(2)}) copy-start(f32[128,2048]{1,0:T(8,128)S(1)} %get-tuple-element.238) | copy-start | bytes 3145732
  95.6 195.2 %copy-start.5 = (s32[128]{0:T(128)S(1)}, s32[128]{0:T(128)}, u32[]{:S(2)}) copy-start(s32[128]{0:T(128)} %param.15) | copy-start | bytes 1540
  96.7 365.0 %reduce-scatter.2.cloned.1.call-start = ((), (), s32[]{:S(2)}) async-start(), calls=%async_computation.2 | async-start | bytes 1081344 | tf_op jit(solution)/shard_map/reduce_scatter | solution.py:142
  290.8 3.2 copy-start
  290.8 3.3 copy-start.2
Sparse Core Ops, SparseCore 0:
  9.9 62.5 all-gather.1
  96.8 193.9 all-reduce.2
  319.9 141.7 reduce-scatter.1
where the time goes:
time: 522 us; the launch traced here: 521 us
  waiting for transfers between devices  338 us (65%)
  blocking collectives  101 us (19%)
  matrix products  32.7 us (6%)
  other arithmetic  22 us (4%)
  between operations  13.9 us (3%)
  local copies, waits for them, and re-layouts  12 us (2%)
    psum x1, waiting for transfers between devices, body(): target, logits = lax.psum((target_part, logit_part), 'head')  194 us
    reduce_scatter x1, waiting for transfers between devices, body(): owned = lax.psum_scatter(key_term, 'seq', scatter_dimension=0, tiled=True)  140 us
    psum x1, blocking collectives, body(): key_grad = lax.psum(owned, 'head')  52.7 us
    all_gather x1, blocking collectives, body(): collected = lax.all_gather(index_keys, 'seq', axis=0, tiled=True)  48.6 us
    dot_general x1, matrix products, latent_scores(): lax.dot_general(portion, flat, (((1,), (1,)), ((), ())), preferred_elemen...  10.9 us
    dot_general x8, matrix products, one_span(): jnp.einsum('thd,kd->thk', index_queries, portion, preferred_element_type=...  10.9 us
  transfers between devices with their start and end apart: 3, of which 3 were waited for; matrix products, arithmetic and copies ran while one was open for 3% of the time, Pallas kernels for 0%

commit v1 on v0

v1 whole, which is shorter than its diff:
```python
import functools

import jax
import jax.numpy as jnp
from jax import lax
from jax.experimental import pallas as pl
from jax.experimental.pallas import tpu as pltpu
from jax.sharding import Mesh, PartitionSpec as P

MLA_HEADS = 128
INDEX_HEADS = 64
LOG2E = 1.4426950408889634
mla_scale = 192.0 ** (-0.5)
loss_weight = 16.0
neg_fill = -1e30

SEQ = ("y", "z", "c")
HEAD = ("x", "w")
f32 = jnp.float32
bf16 = jnp.bfloat16
HELD = pl.BlockSpec(memory_space=pltpu.VMEM)
ANYWHERE = pl.BlockSpec(memory_space=pl.ANY)
SCALARS = pl.BlockSpec(memory_space=pltpu.SMEM)


def target_kernel(skip, base_ref, q_ref, vis_ref, *refs):
    blocks = refs[:-8]
    out_ref, index_ref, bias_ref, s_ref, p_ref, sum_ref, turn_ref, out_sem = refs[-8:]
    heads, depth, rows = q_ref.shape
    key_count = bias_ref.shape[0]
    unit = key_count // base_ref.shape[0]
    span = key_count // len(blocks)
    pairs = heads // 2
    factor = mla_scale * LOG2E

    seen = vis_ref[...]
    for i in range(key_count // unit):
        ids = lax.broadcasted_iota(jnp.int32, (unit, rows), 0) + base_ref[i]
        bias_ref[i * unit : (i + 1) * unit] = jnp.where(ids < seen, 0.0, neg_fill)

    tops, shares = {}, {}
    for step in range(pairs + 2):
        top, total = None, None
        for start in range(0, key_count, span):
            part = slice(start, start + span)
            if step < pairs:
                block = blocks[start // span]
                if step == 0:
                    index_ref[part] = block[:, :skip]
                q = jnp.concatenate([q_ref[2 * step], q_ref[2 * step + 1]], axis=1)
                bias = bias_ref[part]
                s = jnp.dot(block[:, skip : skip + depth], q, preferred_element_type=f32)
                s = s + jnp.concatenate([bias, bias], axis=1)
                s_ref[step % 2, part] = s
                high = jnp.max(s, axis=0, keepdims=True)
                top = high if top is None else jnp.maximum(top, high)
            if 0 <= step - 1 < pairs:
                p = jnp.exp2(s_ref[(step - 1) % 2, part] * factor - tops[step - 1])
                p_ref[(step - 1) % 2, part] = p
                add = jnp.sum(p, axis=0, keepdims=True)
                total = add if total is None else total + add
            if 0 <= step - 2:
                p = p_ref[step % 2, part] * shares[step - 2]
                p = p[:, :rows] + p[:, rows:]
                if step == 2:
                    sum_ref[part] = p
                else:
                    sum_ref[part] += p
        if top is not None:
            tops[step] = top * factor
        if total is not None:
            shares[step - 1] = 1.0 / (total * MLA_HEADS)
    stores = []
    for i in range(key_count // span):
        for start in range(i * span, (i + 1) * span, rows):
            turn_ref[:, start : start + rows] = sum_ref[start : start + rows].T.astype(bf16)
        part = pl.ds(i * span, span)
        stores.append(pltpu.make_async_copy(turn_ref.at[:, part], out_ref.at[:, part], out_sem.at[i]))
        stores[-1].start()
    for store in stores:
        store.wait()


def head_target(queries, blocks, visible, base, skip):
    row_count, heads, depth = queries.shape
    key_count = sum(block.shape[0] for block in blocks)
    turned = queries.transpose(1, 2, 0)
    visible = visible.reshape(1, row_count)
    outs = (
        jax.ShapeDtypeStruct((row_count, key_count), bf16),
        jax.ShapeDtypeStruct((key_count, skip), bf16),
    )
    return pl.pallas_call(
        functools.partial(target_kernel, skip),
        in_specs=[SCALARS] + [HELD] * (2 + len(blocks)),
        out_specs=[ANYWHERE, HELD],
        out_shape=outs,
        scratch_shapes=[
            pltpu.VMEM((key_count, row_count), f32),
            pltpu.VMEM((2, key_count, 2 * row_count), f32),
            pltpu.VMEM((2, key_count, 2 * row_count), f32),
            pltpu.VMEM((key_count, row_count), f32),
            pltpu.VMEM((row_count, key_count), bf16),
            pltpu.SemaphoreType.DMA((len(blocks),)),
        ],
        compiler_params=pltpu.CompilerParams(vmem_limit_bytes=20 << 20),
        name="head_target",
    )(base, turned, visible, *blocks)


def pack_kernel(iq_ref, w_ref, out_ref):
    groups, count, depth = iq_ref.shape
    line = lax.broadcasted_iota(jnp.int32, (16, depth), 0)
    for g in range(groups):
        out_ref[g, :count] = iq_ref[g]
        w = w_ref[g : g + 1]
        high = w.astype(bf16).astype(f32)
        mid = (w - high).astype(bf16).astype(f32)
        low = w - high - mid
        lines = jnp.where(line == 0, high, jnp.where(line == 1, mid, jnp.where(line == 2, low, 0.0)))
        out_ref[g, count:] = lines.astype(bf16)


def pack_index(iq, weights):
    groups, count, depth = iq.shape
    return pl.pallas_call(
        pack_kernel,
        in_specs=[HELD] * 2,
        out_specs=HELD,
        out_shape=jax.ShapeDtypeStruct((groups, count + 16, depth), bf16),
        name="pack_index",
    )(iq, weights)


def unpack(got_ref, q_ref, w_ref):
    groups, lines, depth = got_ref.shape
    count = lines - 16
    for g in range(groups):
        piece = slice(g * count, (g + 1) * count)
        q_ref[piece] = got_ref[g, :count]
        w = jnp.sum(got_ref[g, count:].astype(f32), axis=0, keepdims=True)
        w = w * (INDEX_HEADS * depth) ** (-0.5)
        w_ref[piece] = jnp.broadcast_to(w, (depth, count)).T


def prob_kernel(shape, got_ref, k_ref, vis_ref, kid_ref, out_ref, q_ref, w_ref):
    groups, rows, heads = shape
    span = 512
    unpack(got_ref, q_ref, w_ref)
    w = w_ref[:, :1]
    for start in range(0, k_ref.shape[0], span):
        prod = lax.dot_general(
            q_ref[...], k_ref[start : start + span], (((1,), (1,)), ((), ())), preferred_element_type=f32
        )
        part = jnp.maximum(prod, 0.0) * w
        part = part.reshape(groups, rows, heads, span)
        part = jnp.sum(jnp.sum(part, axis=0), axis=1)
        out_ref[:, start : start + span] = part
    logits = jnp.where(kid_ref[...] < vis_ref[...], out_ref[...], neg_fill)
    peak = jnp.max(logits, axis=1, keepdims=True)
    e = jnp.exp2((logits - peak) * LOG2E)
    out_ref[...] = e * (1.0 / jnp.sum(e, axis=1, keepdims=True))


def index_prob(got, keys, visible, key_ids, shape):
    groups, rows, heads = shape
    key_count, depth = keys.shape
    count = groups * rows * heads
    return pl.pallas_call(
        functools.partial(prob_kernel, shape),
        in_specs=[HELD] * 4,
        out_specs=HELD,
        out_shape=jax.ShapeDtypeStruct((rows, key_count), f32),
        scratch_shapes=[pltpu.VMEM((count, depth), bf16), pltpu.VMEM((count, depth), f32)],
        compiler_params=pltpu.CompilerParams(vmem_limit_bytes=20 << 20),
        name="index_prob",
    )(got, keys, visible, key_ids)


def edges(shape, q, k, prob_ref, part_ref, start):
    groups, rows, heads = shape
    span = k.shape[0]
    prod = lax.dot_general(q, k, (((1,), (1,)), ((), ())), preferred_element_type=f32)
    target = jnp.sum(part_ref[:, :, start : start + span].astype(f32), axis=0)
    grad = loss_weight * (prob_ref[:, start : start + span] - target)
    wide = jnp.broadcast_to(grad[None, :, None, :], (groups, rows, heads, span))
    return jnp.where(prod > 0.0, wide.reshape(q.shape[0], span), 0.0).astype(bf16)


def key_kernel(shape, unit, slot_ref, got_ref, k_ref, prob_ref, part_ref, kg_ref, q_ref, w_ref):
    span = 512
    unpack(got_ref, q_ref, w_ref)
    q = q_ref[...]
    lift = (q.astype(f32) * w_ref[...]).T.astype(bf16)
    for start in range(0, k_ref.shape[0], span):
        edge = edges(shape, q, k_ref[start : start + span], prob_ref, part_ref, start)
        turned = jnp.dot(lift, edge, preferred_element_type=f32).T
        for i in range(span // unit):
            kg_ref[slot_ref[start // unit + i]] = turned[i * unit : (i + 1) * unit]


def query_kernel(shape, got_ref, k_ref, prob_ref, part_ref, dq_ref, acc_ref, q_ref, w_ref):
    groups, rows, heads = shape
    depth = k_ref.shape[1]
    span = 512
    unpack(got_ref, q_ref, w_ref)
    q = q_ref[...]
    for start in range(0, k_ref.shape[0], span):
        k = k_ref[start : start + span]
        edge = edges(shape, q, k, prob_ref, part_ref, start)
        step = jnp.dot(edge, k, preferred_element_type=f32)
        if start == 0:
            acc_ref[...] = step
        else:
            acc_ref[...] += step
    acc = acc_ref[...]
    group_rows = rows * heads
    scale = (INDEX_HEADS * depth) ** (-0.5)
    dq = (acc * w_ref[...]).astype(bf16)
    own = acc * q.astype(f32)
    line = lax.broadcasted_iota(jnp.int32, (16, group_rows), 0)
    for g in range(groups):
        piece = slice(g * group_rows, (g + 1) * group_rows)
        dq_ref[g, :group_rows] = dq[piece]
        dw = jnp.sum(own[piece].T, axis=0, keepdims=True) * scale
        high = dw.astype(bf16).astype(f32)
        mid = (dw - high).astype(bf16).astype(f32)
        low = dw - high - mid
        dq_ref[g, group_rows:] = jnp.where(
            line == 0, high, jnp.where(line == 1, mid, jnp.where(line == 2, low, 0.0))
        ).astype(bf16)


def key_backward(slots, got, keys, prob, parts, shape, unit):
    groups, rows, heads = shape
    key_count, depth = keys.shape
    count = groups * rows * heads
    return pl.pallas_call(
        functools.partial(key_kernel, shape, unit),
        in_specs=[SCALARS] + [HELD] * 4,
        out_specs=HELD,
        out_shape=jax.ShapeDtypeStruct((key_count // unit, unit, depth), f32),
        scratch_shapes=[pltpu.VMEM((count, depth), bf16), pltpu.VMEM((count, depth), f32)],
        compiler_params=pltpu.CompilerParams(vmem_limit_bytes=20 << 20),
        name="key_backward",
    )(slots, got, keys, prob, parts)


def query_backward(got, keys, prob, parts, shape):
    groups, rows, heads = shape
    depth = keys.shape[1]
    count = groups * rows * heads
    return pl.pallas_call(
        functools.partial(query_kernel, shape),
        in_specs=[HELD] * 4,
        out_specs=HELD,
        out_shape=jax.ShapeDtypeStruct((groups, rows * heads + 16, depth), bf16),
        scratch_shapes=[
            pltpu.VMEM((count, depth), f32),
            pltpu.VMEM((count, depth), bf16),
            pltpu.VMEM((count, depth), f32),
        ],
        compiler_params=pltpu.CompilerParams(vmem_limit_bytes=20 << 20),
        name="query_backward",
    )(got, keys, prob, parts)


def take(a, axis, shift):
    n = lax.axis_size(axis)
    return lax.ppermute(a, axis, [((i + shift) % n, i) for i in range(n)])


def take_z(a, shift):
    place = lambda i: i % 4 * 2 + i % 8 // 4
    return lax.ppermute(a, ("z", "w"), [(place(i + shift), place(i)) for i in range(8)])


def gather_keys(shard, sent):
    found = (take_z(shard, 1), take_z(shard, -1), take_z(shard, 2), sent)
    z1, z3, z2, sent = lax.optimization_barrier(found)
    row = jnp.concatenate([shard, z1, z2, z3], axis=0)
    row, sent = lax.optimization_barrier((row, sent))
    blocks = [row, take(row, "y", 1), take(row, "y", -1), take(row, "y", 2)]
    blocks += [take(block, "c", 1) for block in blocks]
    return blocks, [(dy, dz) for dy in (0, 1, 3, 2) for dz in range(4)], sent


def add_up(own, moved):
    moved = lax.optimization_barrier(moved)
    return own.astype(f32) + moved[0].astype(f32) + moved[1].astype(f32) + moved[2].astype(f32)


def pair_sum(kg, unit):
    own = kg.shape[0] // 2
    kg = kg[:own] + take(kg[own:], "c", 1)
    return kg.astype(bf16).reshape(4, 4, unit, kg.shape[-1])


def ring_sum(kg):
    kg = add_up(kg[0], (take(kg[1], "y", -1), take(kg[3], "y", 1), take(kg[2], "y", 2)))
    kg = kg.astype(bf16)
    return add_up(kg[0], (take_z(kg[1], -1), take_z(kg[3], 1), take_z(kg[2], 2)))


def body(latent_queries, latent_keys, index_queries, index_keys, head_weights, visible):
    row_count = latent_queries.shape[0]
    unit = latent_keys.shape[0]
    depth = index_keys.shape[1]
    index_heads = index_queries.shape[1]
    groups = lax.axis_size(HEAD)
    rows = row_count // groups
    me = lax.axis_index(HEAD)
    core = lax.axis_index("c")

    count = rows * index_heads
    sent = pack_index(index_queries.reshape(groups, count, depth), head_weights.reshape(groups, count))
    fill = jnp.zeros((unit, -(depth + latent_keys.shape[1]) % 128), bf16)
    blocks, places, sent = gather_keys(jnp.concatenate([index_keys, latent_keys, fill], axis=1), sent)
    chips = len(places)
    key_count = 2 * chips * unit
    dy, dz = (jnp.array([p[i] for p in places], jnp.int32) for i in range(2))
    chip = (lax.axis_index("y") + dy) % 4 * 4 + (lax.axis_index("z") + dz) % 4
    slots = jnp.concatenate([dy * 4 + dz, chips + dy * 4 + dz])
    base = jnp.concatenate([chip * 2 + core, chip * 2 + 1 - core]) * unit
    key_ids = (base[:, None] + jnp.arange(unit, dtype=jnp.int32)[None]).reshape(1, key_count)
    got = lax.all_to_all(sent, HEAD, split_axis=0, concat_axis=0, tiled=True)
    my_visible = lax.dynamic_slice_in_dim(visible, me * rows, rows, 0).reshape(rows, 1)
    shape = (groups, rows, index_heads)

    part, keys = head_target(latent_queries, blocks, visible, base, depth)
    parts = lax.all_to_all(
        part.reshape(groups, rows, key_count), HEAD, split_axis=0, concat_axis=0, tiled=True
    )
    prob = index_prob(got, keys, my_visible, key_ids, shape)
    kg = pair_sum(key_backward(slots, got, keys, prob, parts, shape, unit), unit)
    kg, prob = lax.optimization_barrier((kg, prob))
    dq = query_backward(got, keys, prob, parts, shape)
    kg = ring_sum(kg)
    high = kg.astype(bf16)
    low = (kg - high.astype(f32)).astype(bf16)
    kg = jnp.broadcast_to(jnp.concatenate([high, low], axis=0)[None], (groups, 2 * unit, depth))
    back = jnp.concatenate([dq, kg], axis=1)
    back = lax.all_to_all(back, HEAD, split_axis=0, concat_axis=0, tiled=True)
    query_grad = back[:, :count].reshape(row_count, index_heads, depth)
    weight_grad = jnp.sum(back[:, count : count + 16].astype(f32), axis=1)
    copies = back[:, count + 16 :].astype(f32)
    key_grad = jnp.sum(copies[:, :unit] + copies[:, unit:], axis=0)
    return query_grad, weight_grad.reshape(row_count, index_heads), key_grad


def solution(mesh):
    fine = Mesh(mesh.devices.reshape(4, 4, 2, 4, 2), ("y", "z", "c", "x", "w"))
    placed = (
        P(SEQ, HEAD, None),
        P(SEQ, None),
        P(SEQ, HEAD, None),
        P(SEQ, None),
        P(SEQ, HEAD),
        P(SEQ),
    )
    return jax.shard_map(
        body,
        mesh=fine,
        in_specs=placed,
        out_specs=(P(SEQ, HEAD, None), P(SEQ, HEAD), P(SEQ, None)),
        check_vma=False,
    )
```

time: 522 us -> 123 us (0.24)
  the two profiles are of different devices: /device:TPU:0 before, /device:TPU:64 now
where the time goes in v1:
time: 123 us
  waiting for transfers between devices  40.7 us (33%)
  starting transfers between devices  32.5 us (26%)
  blocking collectives  21.6 us (18%)
  Pallas kernels  19 us (15%)
  local copies, waits for them, and re-layouts  4.24 us (3%)
  other arithmetic  3.7 us (3%)
    all_to_all x1, blocking collectives, body(): back = lax.all_to_all(back, HEAD, split_axis=0, concat_axis=0, tiled=True)  21.6 us
    ppermute x11, waiting for transfers between devices, take(): return lax.ppermute(a, axis, [((i + shift) % n, i) for i in range(n)])  18 us
    all_to_all x1, waiting for transfers between devices, body(): lax.all_to_all(part.reshape(groups, rows, key_count), HEAD, split_axis=0,...  18 us
    pallas_call x1, Pallas kernels, head_target(): pl.pallas_call(functools.partial(target_kernel, skip), in_specs=[SCALARS]...  10.6 us
    ppermute x11, starting transfers between devices, take(): return lax.ppermute(a, axis, [((i + shift) % n, i) for i in range(n)])  9.18 us
    ppermute x6, starting transfers between devices, take_z(): lax.ppermute(a, ('z', 'w'), [(place(i + shift), place(i)) for i in range(...  8.39 us
    all_to_all x1, starting transfers between devices, body(): lax.all_to_all(part.reshape(groups, rows, key_count), HEAD, split_axis=0,...  7.62 us
    all_to_all x1, starting transfers between devices, body(): got = lax.all_to_all(sent, HEAD, split_axis=0, concat_axis=0, tiled=True)  7.35 us
  transfers between devices with their start and end apart: 19, of which 11 were waited for; matrix products, arithmetic and copies ran while one was open for 2% of the time, Pallas kernels for 13%

profile of v1, /device:TPU:64, one launch (start us, length us, event | category | flops | bytes accessed | tf_op | source)
XLA Modules:
  0.0 122.6 jit_solution(15006861725402857634)
XLA Ops:
  1.8 1.9 %collective-permute-start.1 = (bf16[64,768]{1,0:T(8,128)(2,1)S(1)}, bf16[64,768]{1,0:T(8,128)(2,1)S(1)}, u32[]{:S(2)}, u32[]{:S(2)}) collective-permute-start(bf16[64,768]{1,0:T(8,128)(2,1)S(1)} %pad_maximum_fusion.2), channel_id=1, source_target_pairs={{49,0},{0,16},{16,32},{32,48},{48,1},{1,17},{17,33},{33,49},{51,2}... | collective-permute-start | bytes 294920 | tf_op jit(solution)/shard_map/ppermute | solution.py:275
  3.8 3.5 %collective-permute-start.2 = (bf16[64,768]{1,0:T(8,128)(2,1)S(1)}, bf16[64,768]{1,0:T(8,128)(2,1)S(1)}, u32[]{:S(2)}, u32[]{:S(2)}) collective-permute-start(bf16[64,768]{1,0:T(8,128)(2,1)S(1)} %pad_maximum_fusion.2), channel_id=1, source_target_pairs={{32,0},{48,16},{1,32},{17,48},{33,1},{49,17},{0,33},{16,49},{34,2}... | collective-permute-start | bytes 294920 | tf_op jit(solution)/shard_map/ppermute | solution.py:275
  8.7 1.7 %pack_index.1 = bf16[8,144,128]{2,1,0:T(8,128)(2,1)} custom-call(bf16[8,128,128]{2,1,0:T(8,128)(2,1)} %bitcast.39, f32[8,128]{1,0:T(8,128)} %reshape.74.w_ref), custom_call_target="tpu_custom_call" | custom-call | tf_op jit(solution)/shard_map/pack_index/pallas_call | solution.py:126
  10.4 2.1 %collective-permute-done.2 = bf16[64,768]{1,0:T(8,128)(2,1)S(1)} collective-permute-done((bf16[64,768]{1,0:T(8,128)(2,1)S(1)}, bf16[64,768]{1,0:T(8,128)(2,1)S(1)}, u32[]{:S(2)}, u32[]{:S(2)}) %collective-permute-start.2) | collective-permute-done | bytes 98336 | tf_op jit(solution)/shard_map/ppermute | solution.py:275
  13.5 3.1 %collective-permute-start.3 = (bf16[256,768]{1,0:T(8,128)(2,1)S(1)}, bf16[256,768]{1,0:T(8,128)(2,1)S(1)}, u32[]{:S(2)}, u32[]{:S(2)}) collective-permute-start(bf16[256,768]{1,0:T(8,128)(2,1)S(1)} %pad_maximum_fusion.1.refs_0_), channel_id=1, source_target_pairs={{64,0},{128,64},{192,128},{0,192},{65,1},{129,65},{193,129},{1,193... | collective-permute-start | bytes 1179656 | tf_op jit(solution)/shard_map/ppermute | solution.py:270
  16.5 2.2 %collective-permute-start.5 = (bf16[256,768]{1,0:T(8,128)(2,1)S(1)}, bf16[256,768]{1,0:T(8,128)(2,1)S(1)}, u32[]{:S(2)}, u32[]{:S(2)}) collective-permute-start(bf16[256,768]{1,0:T(8,128)(2,1)S(1)} %pad_maximum_fusion.1.refs_0_), channel_id=1, source_target_pairs={{128,0},{192,64},{0,128},{64,192},{129,1},{193,65},{1,129},{65,193... | collective-permute-start | bytes 1179656 | tf_op jit(solution)/shard_map/ppermute | solution.py:270
  18.7 7.3 %all-to-all-start = ((bf16[8,144,128]{2,1,0:T(8,128)(2,1)}), bf16[8,144,128]{2,1,0:T(8,128)(2,1)S(1)}, u32[]{:S(2)}, u32[]{:S(2)}) async-start(bf16[8,144,128]{2,1,0:T(8,128)(2,1)} %pack_index.1), calls=%async_computation | async-start | bytes 589824 | tf_op jit(solution)/shard_map/all_to_all | solution.py:326
  26.1 5.3 %collective-permute-done.3.refs_1_ = bf16[256,768]{1,0:T(8,128)(2,1)S(1)} collective-permute-done((bf16[256,768]{1,0:T(8,128)(2,1)S(1)}, bf16[256,768]{1,0:T(8,128)(2,1)S(1)}, u32[]{:S(2)}, u32[]{:S(2)}) %collective-permute-start.3) | collective-permute-done | bytes 393248 | tf_op jit(solution)/shard_map/ppermute | solution.py:270
  31.4 3.4 %collective-permute-done.4.refs_2_ = bf16[256,768]{1,0:T(8,128)(2,1)S(1)} collective-permute-done((bf16[256,768]{1,0:T(8,128)(2,1)S(1)}, bf16[256,768]{1,0:T(8,128)(2,1)S(1)}, u32[]{:S(2)}, u32[]{:S(2)}) %collective-permute-start.4) | collective-permute-done | bytes 393248 | tf_op jit(solution)/shard_map/ppermute | solution.py:270
  35.4 1.1 collective-permute-done.8.refs_6_
  37.1 1.7 %copy-done = bf16[128,16,576]{0,2,1:T(8,128)(2,1)S(1)} copy-done((bf16[128,16,576]{0,2,1:T(8,128)(2,1)S(1)}, bf16[128,16,576]{0,2,1:T(8,128)(2,1)}, u32[]{:S(2)}) %copy-start) | copy-done | bytes 2359320
  38.8 10.6 %head_target.1 = (bf16[128,2048]{1,0:T(8,128)(2,1)}, bf16[2048,128]{1,0:T(8,128)(2,1)S(1)}) custom-call(s32[32]{0:T(128)S(1)} %add_multiply_fusion.base_ref, bf16[16,576,128]{2,1,0:T(8,128)(2,1)S(1)} %bitcast.34, s32[1,128]{1,0:T(1,128)S(1)} %bitcast.35, bf16[256,768]{1,0:T(8,128)(2,1)S(1)} %pad_maximum_fusion.1.refs_0_, ...), custom_call_target="tpu_custom_call" | custom-call | tf_op jit(solution)/shard_map/head_target/pallas_call | solution.py:93
  49.4 7.6 %all-to-all-start.1 = ((bf16[8,16,2048]{2,1,0:T(8,128)(2,1)}), bf16[8,16,2048]{2,1,0:T(8,128)(2,1)S(1)}, u32[]{:S(2)}, u32[]{:S(2)}) async-start(bf16[8,16,2048]{2,1,0:T(8,128)(2,1)} %bitcast.4), calls=%async_computation.1 | async-start | bytes 1048576 | tf_op jit(solution)/shard_map/all_to_all | solution.py:331
  57.3 1.6 %index_prob.1.prob_ref = f32[16,2048]{1,0:T(8,128)S(1)} custom-call(bf16[8,144,128]{2,1,0:T(8,128)(2,1)S(1)} %all-to-all-done.got_ref, bf16[2048,128]{1,0:T(8,128)(2,1)S(1)} %get-tuple-element.25.k_ref, s32[16,1]{1,0:T(8,128)S(1)} %copy.14.vis_ref, s32[1,2048]{1,0:T(1,128)S(1)} %add.114.kid_ref), custom_call_target="tpu_custom_call" | custom-call | tf_op jit(solution)/shard_map/index_prob/pallas_call | solution.py:169
  58.9 18.0 %all-to-all-done.1.part_ref = bf16[8,16,2048]{2,1,0:T(8,128)(2,1)S(1)} async-done(((bf16[8,16,2048]{2,1,0:T(8,128)(2,1)}), bf16[8,16,2048]{2,1,0:T(8,128)(2,1)S(1)}, u32[]{:S(2)}, u32[]{:S(2)}) %all-to-all-start.1) | async-done | bytes 524320 | tf_op jit(solution)/shard_map/all_to_all | solution.py:331
  76.9 2.5 %key_backward.1 = f32[32,64,128]{2,1,0:T(8,128)S(1)} custom-call(s32[32]{0:T(128)S(1)} %copy-done.2, bf16[8,144,128]{2,1,0:T(8,128)(2,1)S(1)} %all-to-all-done.got_ref, bf16[2048,128]{1,0:T(8,128)(2,1)S(1)} %get-tuple-element.25.k_ref, f32[16,2048]{1,0:T(8,128)S(1)} %index_prob.1.prob_ref, bf16[8,16,2048]{2,1,0:T(8,128)(2,1)S(1)} %all-to-all-done.1.part_ref), custom_call_target="tpu_custom_call" | custom-call | tf_op jit(solution)/shard_map/key_backward/pallas_call | solution.py:238
  79.6 1.9 %collective-permute-done.10 = f32[16,64,128]{2,1,0:T(8,128)S(1)} collective-permute-done((f32[16,64,128]{2,1,0:T(8,128)S(1)}, f32[16,64,128]{2,1,0:T(8,128)S(1)}, u32[]{:S(2)}, u32[]{:S(2)}) %collective-permute-start.10) | collective-permute-done | bytes 524320 | tf_op jit(solution)/shard_map/ppermute | solution.py:270
  81.7 3.2 %collective-permute-start.12 = (bf16[4,64,128]{2,1,0:T(8,128)(2,1)S(1)}, bf16[4,64,128]{2,1,0:T(8,128)(2,1)S(1)}, u32[]{:S(2)}, u32[]{:S(2)}) collective-permute-start(bf16[4,64,128]{2,1,0:T(8,128)(2,1)S(1)} %get-tuple-element.43), channel_id=1, source_target_pairs={{64,0},{128,64},{192,128},{0,192},{65,1},{129,65},{193,129},{1,193... | collective-permute-start | bytes 196616 | tf_op jit(solution)/shard_map/ppermute | solution.py:270
  84.9 2.2 %collective-permute-done.11 = bf16[4,64,128]{2,1,0:T(8,128)(2,1)S(1)} collective-permute-done((bf16[4,64,128]{2,1,0:T(8,128)(2,1)S(1)}, bf16[4,64,128]{2,1,0:T(8,128)(2,1)S(1)}, u32[]{:S(2)}, u32[]{:S(2)}) %collective-permute-start.11) | collective-permute-done | bytes 65568 | tf_op jit(solution)/shard_map/ppermute | solution.py:270
  87.7 3.0 %collective-permute-done.13 = bf16[4,64,128]{2,1,0:T(8,128)(2,1)S(1)} collective-permute-done((bf16[4,64,128]{2,1,0:T(8,128)(2,1)S(1)}, bf16[4,64,128]{2,1,0:T(8,128)(2,1)S(1)}, u32[]{:S(2)}, u32[]{:S(2)}) %collective-permute-start.13) | collective-permute-done | bytes 65568 | tf_op jit(solution)/shard_map/ppermute | solution.py:270
  90.8 2.0 %collective-permute-start.15 = (bf16[64,128]{1,0:T(8,128)(2,1)S(1)}, bf16[64,128]{1,0:T(8,128)(2,1)S(1)}, u32[]{:S(2)}, u32[]{:S(2)}) collective-permute-start(bf16[64,128]{1,0:T(8,128)(2,1)S(1)} %get-tuple-element.48), channel_id=1, source_target_pairs={{16,0},{32,16},{48,32},{1,48},{17,1},{33,17},{49,33},{0,49},{18,2}... | collective-permute-start | bytes 49160 | tf_op jit(solution)/shard_map/ppermute | solution.py:275
  93.6 2.5 %query_backward.1 = bf16[8,144,128]{2,1,0:T(8,128)(2,1)S(1)} custom-call(bf16[8,144,128]{2,1,0:T(8,128)(2,1)S(1)} %all-to-all-done.got_ref, bf16[2048,128]{1,0:T(8,128)(2,1)S(1)} %get-tuple-element.25.k_ref, f32[16,2048]{1,0:T(8,128)S(1)} %index_prob.1.prob_ref, bf16[8,16,2048]{2,1,0:T(8,128)(2,1)S(1)} %all-to-all-done.1.part_ref), custom_call_target="tpu_custom_call" | custom-call | tf_op jit(solution)/shard_map/query_backward/pallas_call | solution.py:253
  96.1 2.6 %collective-permute-done.16 = bf16[64,128]{1,0:T(8,128)(2,1)S(1)} collective-permute-done((bf16[64,128]{1,0:T(8,128)(2,1)S(1)}, bf16[64,128]{1,0:T(8,128)(2,1)S(1)}, u32[]{:S(2)}, u32[]{:S(2)}) %collective-permute-start.16) | collective-permute-done | bytes 16416 | tf_op jit(solution)/shard_map/ppermute | solution.py:275
  98.8 21.6 %all_to_all.15 = bf16[8,272,128]{2,1,0:T(8,128)(2,1)S(1)} all-to-all(bf16[8,272,128]{2,1,0:T(8,128)(2,1)S(1)} %pad_maximum_fusion), channel_id=1, replica_groups=mesh['y'=4,'z'=4,'c'=2,'x'=4,'w'=2] {'x','w'}, dimensions={0} | all-to-all | bytes 1114112 | tf_op jit(solution)/shard_map/all_to_all | solution.py:343
  (56 shorter events, 9.1 us)
Async XLA Ops:
  0.6 34.7 %copy-start.3 = (s32[16]{0:T(128)S(1)}, s32[16]{0:T(128)}, u32[]{:S(2)}) copy-start(s32[16]{0:T(128)} %constant.62.clone) | copy-start | bytes 196
  0.7 34.7 %copy-start.4 = (s32[16]{0:T(128)S(1)}, s32[16]{0:T(128)}, u32[]{:S(2)}) copy-start(s32[16]{0:T(128)} %constant.61.clone) | copy-start | bytes 196
  1.6 35.4 %copy-start.1 = (s32[128]{0:T(128)S(1)}, s32[128]{0:T(128)}, u32[]{:S(2)}) copy-start(s32[128]{0:T(128)} %param.13) | copy-start | bytes 1540
  1.6 8.8 %collective-permute-start = (bf16[64,768]{1,0:T(8,128)(2,1)S(1)}, bf16[64,768]{1,0:T(8,128)(2,1)S(1)}, u32[]{:S(2)}, u32[]{:S(2)}) collective-permute-start(bf16[64,768]{1,0:T(8,128)(2,1)S(1)} %pad_maximum_fusion.2), channel_id=1, source_target_pairs={{16,0},{32,16},{48,32},{1,48},{17,1},{33,17},{49,33},{0,49},{18,2}... | collective-permute-start | bytes 294920 | tf_op jit(solution)/shard_map/ppermute | solution.py:275
  1.8 8.6 %collective-permute-start.1 = (bf16[64,768]{1,0:T(8,128)(2,1)S(1)}, bf16[64,768]{1,0:T(8,128)(2,1)S(1)}, u32[]{:S(2)}, u32[]{:S(2)}) collective-permute-start(bf16[64,768]{1,0:T(8,128)(2,1)S(1)} %pad_maximum_fusion.2), channel_id=1, source_target_pairs={{49,0},{0,16},{16,32},{32,48},{48,1},{1,17},{17,33},{33,49},{51,2}... | collective-permute-start | bytes 294920 | tf_op jit(solution)/shard_map/ppermute | solution.py:275
  3.8 8.7 %collective-permute-start.2 = (bf16[64,768]{1,0:T(8,128)(2,1)S(1)}, bf16[64,768]{1,0:T(8,128)(2,1)S(1)}, u32[]{:S(2)}, u32[]{:S(2)}) collective-permute-start(bf16[64,768]{1,0:T(8,128)(2,1)S(1)} %pad_maximum_fusion.2), channel_id=1, source_target_pairs={{32,0},{48,16},{1,32},{17,48},{33,1},{49,17},{0,33},{16,49},{34,2}... | collective-permute-start | bytes 294920 | tf_op jit(solution)/shard_map/ppermute | solution.py:275
  13.5 17.9 %collective-permute-start.3 = (bf16[256,768]{1,0:T(8,128)(2,1)S(1)}, bf16[256,768]{1,0:T(8,128)(2,1)S(1)}, u32[]{:S(2)}, u32[]{:S(2)}) collective-permute-start(bf16[256,768]{1,0:T(8,128)(2,1)S(1)} %pad_maximum_fusion.1.refs_0_), channel_id=1, source_target_pairs={{64,0},{128,64},{192,128},{0,192},{65,1},{129,65},{193,129},{1,193... | collective-permute-start | bytes 1179656 | tf_op jit(solution)/shard_map/ppermute | solution.py:270
  16.5 18.3 %collective-permute-start.4 = (bf16[256,768]{1,0:T(8,128)(2,1)S(1)}, bf16[256,768]{1,0:T(8,128)(2,1)S(1)}, u32[]{:S(2)}, u32[]{:S(2)}) collective-permute-start(bf16[256,768]{1,0:T(8,128)(2,1)S(1)} %pad_maximum_fusion.1.refs_0_), channel_id=1, source_target_pairs={{192,0},{0,64},{64,128},{128,192},{193,1},{1,65},{65,129},{129,193... | collective-permute-start | bytes 1179656 | tf_op jit(solution)/shard_map/ppermute | solution.py:270
  16.5 18.3 %collective-permute-start.5 = (bf16[256,768]{1,0:T(8,128)(2,1)S(1)}, bf16[256,768]{1,0:T(8,128)(2,1)S(1)}, u32[]{:S(2)}, u32[]{:S(2)}) collective-permute-start(bf16[256,768]{1,0:T(8,128)(2,1)S(1)} %pad_maximum_fusion.1.refs_0_), channel_id=1, source_target_pairs={{128,0},{192,64},{0,128},{64,192},{129,1},{193,65},{1,129},{65,193... | collective-permute-start | bytes 1179656 | tf_op jit(solution)/shard_map/ppermute | solution.py:270
  18.7 16.7 %collective-permute-start.6 = (bf16[256,768]{1,0:T(8,128)(2,1)S(1)}, bf16[256,768]{1,0:T(8,128)(2,1)S(1)}, u32[]{:S(2)}, u32[]{:S(2)}) collective-permute-start(bf16[256,768]{1,0:T(8,128)(2,1)S(1)} %pad_maximum_fusion.1.refs_0_), channel_id=1, source_target_pairs={{8,0},{0,8},{9,1},{1,9},{10,2},{2,10},{11,3},{3,11},{12,4},{4,12},... | collective-permute-start | bytes 1179656 | tf_op jit(solution)/shard_map/ppermute | solution.py:270
  18.7 30.6 %all-to-all-start = ((bf16[8,144,128]{2,1,0:T(8,128)(2,1)}), bf16[8,144,128]{2,1,0:T(8,128)(2,1)S(1)}, u32[]{:S(2)}, u32[]{:S(2)}) async-start(bf16[8,144,128]{2,1,0:T(8,128)(2,1)} %pack_index.1), calls=%async_computation | async-start | bytes 589824 | tf_op jit(solution)/shard_map/all_to_all | solution.py:326
  31.4 4.0 %collective-permute-start.7 = (bf16[256,768]{1,0:T(8,128)(2,1)S(1)}, bf16[256,768]{1,0:T(8,128)(2,1)S(1)}, u32[]{:S(2)}, u32[]{:S(2)}) collective-permute-start(bf16[256,768]{1,0:T(8,128)(2,1)S(1)} %collective-permute-done.3.refs_1_), channel_id=1, source_target_pairs={{8,0},{0,8},{9,1},{1,9},{10,2},{2,10},{11,3},{3,11},{12,4},{4,12},... | collective-permute-start | bytes 1179656 | tf_op jit(solution)/shard_map/ppermute | solution.py:270
  34.8 1.7 %collective-permute-start.8 = (bf16[256,768]{1,0:T(8,128)(2,1)S(1)}, bf16[256,768]{1,0:T(8,128)(2,1)S(1)}, u32[]{:S(2)}, u32[]{:S(2)}) collective-permute-start(bf16[256,768]{1,0:T(8,128)(2,1)S(1)} %collective-permute-done.4.refs_2_), channel_id=1, source_target_pairs={{8,0},{0,8},{9,1},{1,9},{10,2},{2,10},{11,3},{3,11},{12,4},{4,12},... | collective-permute-start | bytes 1179656 | tf_op jit(solution)/shard_map/ppermute | solution.py:270
  34.8 2.3 %collective-permute-start.9 = (bf16[256,768]{1,0:T(8,128)(2,1)S(1)}, bf16[256,768]{1,0:T(8,128)(2,1)S(1)}, u32[]{:S(2)}, u32[]{:S(2)}) collective-permute-start(bf16[256,768]{1,0:T(8,128)(2,1)S(1)} %collective-permute-done.5.refs_3_), channel_id=1, source_target_pairs={{8,0},{0,8},{9,1},{1,9},{10,2},{2,10},{11,3},{3,11},{12,4},{4,12},... | collective-permute-start | bytes 1179656 | tf_op jit(solution)/shard_map/ppermute | solution.py:270
  37.1 1.7 %copy-start = (bf16[128,16,576]{0,2,1:T(8,128)(2,1)S(1)}, bf16[128,16,576]{0,2,1:T(8,128)(2,1)}, u32[]{:S(2)}) copy-start(bf16[128,16,576]{0,2,1:T(8,128)(2,1)} %param.8) | copy-start | bytes 7077892
  49.4 27.6 %copy-start.2 = (s32[32]{0:T(128)S(1)}, s32[32]{0:T(128)}, u32[]{:S(2)}) copy-start(s32[32]{0:T(128)} %constant.67.slot_ref) | copy-start | bytes 388
  49.4 27.5 %all-to-all-start.1 = ((bf16[8,16,2048]{2,1,0:T(8,128)(2,1)}), bf16[8,16,2048]{2,1,0:T(8,128)(2,1)S(1)}, u32[]{:S(2)}, u32[]{:S(2)}) async-start(bf16[8,16,2048]{2,1,0:T(8,128)(2,1)} %bitcast.4), calls=%async_computation.1 | async-start | bytes 1048576 | tf_op jit(solution)/shard_map/all_to_all | solution.py:331
  79.5 2.0 %collective-permute-start.10 = (f32[16,64,128]{2,1,0:T(8,128)S(1)}, f32[16,64,128]{2,1,0:T(8,128)S(1)}, u32[]{:S(2)}, u32[]{:S(2)}) collective-permute-start(f32[16,64,128]{2,1,0:T(8,128)S(1)} %slice.61), channel_id=1, source_target_pairs={{8,0},{0,8},{9,1},{1,9},{10,2},{2,10},{11,3},{3,11},{12,4},{4,12},... | collective-permute-start | bytes 1572872 | tf_op jit(solution)/shard_map/ppermute | solution.py:270
  81.6 5.6 %collective-permute-start.11 = (bf16[4,64,128]{2,1,0:T(8,128)(2,1)S(1)}, bf16[4,64,128]{2,1,0:T(8,128)(2,1)S(1)}, u32[]{:S(2)}, u32[]{:S(2)}) collective-permute-start(bf16[4,64,128]{2,1,0:T(8,128)(2,1)S(1)} %get-tuple-element.44), channel_id=1, source_target_pairs={{192,0},{0,64},{64,128},{128,192},{193,1},{1,65},{65,129},{129,193... | collective-permute-start | bytes 196616 | tf_op jit(solution)/shard_map/ppermute | solution.py:270
  81.7 6.0 %collective-permute-start.12 = (bf16[4,64,128]{2,1,0:T(8,128)(2,1)S(1)}, bf16[4,64,128]{2,1,0:T(8,128)(2,1)S(1)}, u32[]{:S(2)}, u32[]{:S(2)}) collective-permute-start(bf16[4,64,128]{2,1,0:T(8,128)(2,1)S(1)} %get-tuple-element.43), channel_id=1, source_target_pairs={{64,0},{128,64},{192,128},{0,192},{65,1},{129,65},{193,129},{1,193... | collective-permute-start | bytes 196616 | tf_op jit(solution)/shard_map/ppermute | solution.py:270
  84.9 5.8 %collective-permute-start.13 = (bf16[4,64,128]{2,1,0:T(8,128)(2,1)S(1)}, bf16[4,64,128]{2,1,0:T(8,128)(2,1)S(1)}, u32[]{:S(2)}, u32[]{:S(2)}) collective-permute-start(bf16[4,64,128]{2,1,0:T(8,128)(2,1)S(1)} %get-tuple-element.42), channel_id=1, source_target_pairs={{128,0},{192,64},{0,128},{64,192},{129,1},{193,65},{1,129},{65,193... | collective-permute-start | bytes 196616 | tf_op jit(solution)/shard_map/ppermute | solution.py:270
  90.8 5.4 %collective-permute-start.14 = (bf16[64,128]{1,0:T(8,128)(2,1)S(1)}, bf16[64,128]{1,0:T(8,128)(2,1)S(1)}, u32[]{:S(2)}, u32[]{:S(2)}) collective-permute-start(bf16[64,128]{1,0:T(8,128)(2,1)S(1)} %get-tuple-element.49), channel_id=1, source_target_pairs={{49,0},{0,16},{16,32},{32,48},{48,1},{1,17},{17,33},{33,49},{51,2}... | collective-permute-start | bytes 49160 | tf_op jit(solution)/shard_map/ppermute | solution.py:275
  90.8 5.3 %collective-permute-start.15 = (bf16[64,128]{1,0:T(8,128)(2,1)S(1)}, bf16[64,128]{1,0:T(8,128)(2,1)S(1)}, u32[]{:S(2)}, u32[]{:S(2)}) collective-permute-start(bf16[64,128]{1,0:T(8,128)(2,1)S(1)} %get-tuple-element.48), channel_id=1, source_target_pairs={{16,0},{32,16},{48,32},{1,48},{17,1},{33,17},{49,33},{0,49},{18,2}... | collective-permute-start | bytes 49160 | tf_op jit(solution)/shard_map/ppermute | solution.py:275
  92.9 5.8 %collective-permute-start.16 = (bf16[64,128]{1,0:T(8,128)(2,1)S(1)}, bf16[64,128]{1,0:T(8,128)(2,1)S(1)}, u32[]{:S(2)}, u32[]{:S(2)}) collective-permute-start(bf16[64,128]{1,0:T(8,128)(2,1)S(1)} %get-tuple-element.47), channel_id=1, source_target_pairs={{32,0},{48,16},{1,32},{17,48},{33,1},{49,17},{0,33},{16,49},{34,2}... | collective-permute-start | bytes 49160 | tf_op jit(solution)/shard_map/ppermute | solution.py:275

commit v2 on v1

--- a/solution.py
+++ b/solution.py
@@ -23,9 +23,9 @@
 SCALARS = pl.BlockSpec(memory_space=pltpu.SMEM)
 
 
-def target_kernel(skip, base_ref, q_ref, vis_ref, *refs):
-    blocks = refs[:-8]
-    out_ref, index_ref, bias_ref, s_ref, p_ref, sum_ref, turn_ref, out_sem = refs[-8:]
+def target_kernel(skip, base_ref, offset_ref, q_ref, vis_ref, *refs):
+    index_ref, bias_ref, s_ref, p_ref, sum_ref, turn_ref, out_sem = refs[-7:]
+    blocks, outs = refs[:-11], refs[-11:-7]
     heads, depth, rows = q_ref.shape
     key_count = bias_ref.shape[0]
     unit = key_count // base_ref.shape[0]
@@ -70,42 +70,43 @@
             tops[step] = top * factor
         if total is not None:
             shares[step - 1] = 1.0 / (total * MLA_HEADS)
+    for start in range(0, key_count, rows):
+        turn_ref[:, start : start + rows] = sum_ref[start : start + rows].T.astype(bf16)
     stores = []
-    for i in range(key_count // span):
-        for start in range(i * span, (i + 1) * span, rows):
-            turn_ref[:, start : start + rows] = sum_ref[start : start + rows].T.astype(bf16)
-        part = pl.ds(i * span, span)
-        stores.append(pltpu.make_async_copy(turn_ref.at[:, part], out_ref.at[:, part], out_sem.at[i]))
-        stores[-1].start()
+    for i, out in enumerate(outs):
+        for j in range(out.shape[0]):
+            number = i * out.shape[0] + j
+            start = pl.multiple_of(offset_ref[number], out.shape[1])
+            source = turn_ref.at[pl.ds(start, out.shape[1])]
+            stores.append(pltpu.make_async_copy(source, out.at[j], out_sem.at[number]))
+            stores[-1].start()
     for store in stores:
         store.wait()
 
 
-def head_target(queries, blocks, visible, base, skip):
+def head_target(queries, blocks, visible, base, offsets, skip):
     row_count, heads, depth = queries.shape
     key_count = sum(block.shape[0] for block in blocks)
     turned = queries.transpose(1, 2, 0)
     visible = visible.reshape(1, row_count)
-    outs = (
-        jax.ShapeDtypeStruct((row_count, key_count), bf16),
-        jax.ShapeDtypeStruct((key_count, skip), bf16),
-    )
+    rows = row_count // offsets.shape[0]
+    outs = [jax.ShapeDtypeStruct((offsets.shape[0] // 4, rows, key_count), bf16)] * 4
     return pl.pallas_call(
         functools.partial(target_kernel, skip),
-        in_specs=[SCALARS] + [HELD] * (2 + len(blocks)),
-        out_specs=[ANYWHERE, HELD],
-        out_shape=outs,
+        in_specs=[SCALARS, SCALARS] + [HELD] * (2 + len(blocks)),
+        out_specs=[ANYWHERE] * 4 + [HELD],
+        out_shape=outs + [jax.ShapeDtypeStruct((key_count, skip), bf16)],
         scratch_shapes=[
             pltpu.VMEM((key_count, row_count), f32),
             pltpu.VMEM((2, key_count, 2 * row_count), f32),
             pltpu.VMEM((2, key_count, 2 * row_count), f32),
             pltpu.VMEM((key_count, row_count), f32),
             pltpu.VMEM((row_count, key_count), bf16),
-            pltpu.SemaphoreType.DMA((len(blocks),)),
+            pltpu.SemaphoreType.DMA((offsets.shape[0],)),
         ],
-        compiler_params=pltpu.CompilerParams(vmem_limit_bytes=20 << 20),
+        compiler_params=pltpu.CompilerParams(vmem_limit_bytes=24 << 20),
         name="head_target",
-    )(base, turned, visible, *blocks)
+    )(base, offsets, turned, visible, *blocks)
 
 
 def pack_kernel(iq_ref, w_ref, out_ref):
@@ -177,29 +178,30 @@
     )(got, keys, visible, key_ids)
 
 
-def edges(shape, q, k, prob_ref, part_ref, start):
+def edges(shape, q, k, prob_ref, near_ref, part_ref, start):
     groups, rows, heads = shape
     span = k.shape[0]
     prod = lax.dot_general(q, k, (((1,), (1,)), ((), ())), preferred_element_type=f32)
-    target = jnp.sum(part_ref[:, :, start : start + span].astype(f32), axis=0)
+    here = slice(start, start + span)
+    target = near_ref[:, here] + part_ref[:, here].astype(f32)
     grad = loss_weight * (prob_ref[:, start : start + span] - target)
     wide = jnp.broadcast_to(grad[None, :, None, :], (groups, rows, heads, span))
     return jnp.where(prod > 0.0, wide.reshape(q.shape[0], span), 0.0).astype(bf16)
 
 
-def key_kernel(shape, unit, slot_ref, got_ref, k_ref, prob_ref, part_ref, kg_ref, q_ref, w_ref):
+def key_kernel(shape, unit, slot_ref, got_ref, k_ref, prob_ref, near_ref, part_ref, kg_ref, q_ref, w_ref):
     span = 512
     unpack(got_ref, q_ref, w_ref)
     q = q_ref[...]
     lift = (q.astype(f32) * w_ref[...]).T.astype(bf16)
     for start in range(0, k_ref.shape[0], span):
-        edge = edges(shape, q, k_ref[start : start + span], prob_ref, part_ref, start)
+        edge = edges(shape, q, k_ref[start : start + span], prob_ref, near_ref, part_ref, start)
         turned = jnp.dot(lift, edge, preferred_element_type=f32).T
         for i in range(span // unit):
             kg_ref[slot_ref[start // unit + i]] = turned[i * unit : (i + 1) * unit]
 
 
-def query_kernel(shape, got_ref, k_ref, prob_ref, part_ref, dq_ref, acc_ref, q_ref, w_ref):
+def query_kernel(shape, got_ref, k_ref, prob_ref, near_ref, part_ref, dq_ref, acc_ref, q_ref, w_ref):
     groups, rows, heads = shape
     depth = k_ref.shape[1]
     span = 512
@@ -207,7 +209,7 @@
     q = q_ref[...]
     for start in range(0, k_ref.shape[0], span):
         k = k_ref[start : start + span]
-        edge = edges(shape, q, k, prob_ref, part_ref, start)
+        edge = edges(shape, q, k, prob_ref, near_ref, part_ref, start)
         step = jnp.dot(edge, k, preferred_element_type=f32)
         if start == 0:
             acc_ref[...] = step
@@ -237,13 +239,13 @@
     count = groups * rows * heads
     return pl.pallas_call(
         functools.partial(key_kernel, shape, unit),
-        in_specs=[SCALARS] + [HELD] * 4,
+        in_specs=[SCALARS] + [HELD] * 5,
         out_specs=HELD,
         out_shape=jax.ShapeDtypeStruct((key_count // unit, unit, depth), f32),
         scratch_shapes=[pltpu.VMEM((count, depth), bf16), pltpu.VMEM((count, depth), f32)],
         compiler_params=pltpu.CompilerParams(vmem_limit_bytes=20 << 20),
         name="key_backward",
-    )(slots, got, keys, prob, parts)
+    )(slots, got, keys, prob, *parts)
 
 
 def query_backward(got, keys, prob, parts, shape):
@@ -252,7 +254,7 @@
     count = groups * rows * heads
     return pl.pallas_call(
         functools.partial(query_kernel, shape),
-        in_specs=[HELD] * 4,
+        in_specs=[HELD] * 5,
         out_specs=HELD,
         out_shape=jax.ShapeDtypeStruct((groups, rows * heads + 16, depth), bf16),
         scratch_shapes=[
@@ -262,7 +264,7 @@
         ],
         compiler_params=pltpu.CompilerParams(vmem_limit_bytes=20 << 20),
         name="query_backward",
-    )(got, keys, prob, parts)
+    )(got, keys, prob, *parts)
 
 
 def take(a, axis, shift):
@@ -280,9 +282,12 @@
     z1, z3, z2, sent = lax.optimization_barrier(found)
     row = jnp.concatenate([shard, z1, z2, z3], axis=0)
     row, sent = lax.optimization_barrier((row, sent))
-    blocks = [row, take(row, "y", 1), take(row, "y", -1), take(row, "y", 2)]
+    y1, y3, y2 = take(row, "y", 1), take(row, "y", -1), take(row, "y", 2)
+    got = lax.all_to_all(sent, HEAD, split_axis=0, concat_axis=0, tiled=True)
+    blocks = [row, y1, y3, y2]
     blocks += [take(block, "c", 1) for block in blocks]
-    return blocks, [(dy, dz) for dy in (0, 1, 3, 2) for dz in range(4)], sent
+    blocks[-1], got = lax.optimization_barrier((blocks[-1], got))
+    return blocks, [(dy, dz) for dy in (0, 1, 3, 2) for dz in range(4)], got
 
 
 def add_up(own, moved):
@@ -315,7 +320,7 @@
     count = rows * index_heads
     sent = pack_index(index_queries.reshape(groups, count, depth), head_weights.reshape(groups, count))
     fill = jnp.zeros((unit, -(depth + latent_keys.shape[1]) % 128), bf16)
-    blocks, places, sent = gather_keys(jnp.concatenate([index_keys, latent_keys, fill], axis=1), sent)
+    blocks, places, got = gather_keys(jnp.concatenate([index_keys, latent_keys, fill], axis=1), sent)
     chips = len(places)
     key_count = 2 * chips * unit
     dy, dz = (jnp.array([p[i] for p in places], jnp.int32) for i in range(2))
@@ -323,28 +328,26 @@
     slots = jnp.concatenate([dy * 4 + dz, chips + dy * 4 + dz])
     base = jnp.concatenate([chip * 2 + core, chip * 2 + 1 - core]) * unit
     key_ids = (base[:, None] + jnp.arange(unit, dtype=jnp.int32)[None]).reshape(1, key_count)
-    got = lax.all_to_all(sent, HEAD, split_axis=0, concat_axis=0, tiled=True)
     my_visible = lax.dynamic_slice_in_dim(visible, me * rows, rows, 0).reshape(rows, 1)
     shape = (groups, rows, index_heads)
 
-    part, keys = head_target(latent_queries, blocks, visible, base, depth)
-    parts = lax.all_to_all(
-        part.reshape(groups, rows, key_count), HEAD, split_axis=0, concat_axis=0, tiled=True
-    )
+    x, w = lax.axis_index("x"), lax.axis_index("w")
+    places = [((x + i) % 4 * 2 + (w + j) % 2) * rows for i in range(4) for j in range(2)]
+    *part, keys = head_target(latent_queries, blocks, visible, base, jnp.stack(places), depth)
+    moved = (take(part[1], "x", -1), take(part[3], "x", 1), take(part[2], "x", 2))
+    near = add_up(part[0], moved)
+    parts = (near[0], take(near[1].astype(bf16), "w", 1))
     prob = index_prob(got, keys, my_visible, key_ids, shape)
     kg = pair_sum(key_backward(slots, got, keys, prob, parts, shape, unit), unit)
     kg, prob = lax.optimization_barrier((kg, prob))
     dq = query_backward(got, keys, prob, parts, shape)
     kg = ring_sum(kg)
-    high = kg.astype(bf16)
-    low = (kg - high.astype(f32)).astype(bf16)
-    kg = jnp.broadcast_to(jnp.concatenate([high, low], axis=0)[None], (groups, 2 * unit, depth))
+    kg = jnp.broadcast_to(kg.astype(bf16)[None], (groups, unit, depth))
     back = jnp.concatenate([dq, kg], axis=1)
     back = lax.all_to_all(back, HEAD, split_axis=0, concat_axis=0, tiled=True)
     query_grad = back[:, :count].reshape(row_count, index_heads, depth)
     weight_grad = jnp.sum(back[:, count : count + 16].astype(f32), axis=1)
-    copies = back[:, count + 16 :].astype(f32)
-    key_grad = jnp.sum(copies[:, :unit] + copies[:, unit:], axis=0)
+    key_grad = jnp.sum(back[:, count + 16 :].astype(f32), axis=0)
     return query_grad, weight_grad.reshape(row_count, index_heads), key_grad
 
 

time: 123 us -> 116 us (0.943)
  waiting for transfers between devices: 40.7 us -> 31.2 us
  starting transfers between devices: 32.5 us -> 35.8 us
  blocking collectives: 21.6 us -> 19.7 us
    all_to_all x2 -> x1, waiting for transfers between devices: 18 us -> 3.81 us  [gather_keys(): got = lax.all_to_all(sent, HEAD, split_axis=0, concat_axis=0, tiled=True)]
    all_to_all x2 -> x1, starting transfers between devices: 15 us -> 7.35 us  [gather_keys(): got = lax.all_to_all(sent, HEAD, split_axis=0, concat_axis=0, tiled=True)]
    ppermute x11 -> x15, starting transfers between devices: 9.18 us -> 16.5 us  [take(): return lax.ppermute(a, axis, [((i + shift) % n, i) for i in range(n)])]
    ppermute x11 -> x15, waiting for transfers between devices: 18 us -> 23.6 us  [take(): return lax.ppermute(a, axis, [((i + shift) % n, i) for i in range(n)])]
    ppermute x6, starting transfers between devices: 8.39 us -> 12 us  [take_z(): lax.ppermute(a, ('z', 'w'), [(place(i + shift), place(i)) for i in range(...]
    all_to_all x1, blocking collectives: 21.6 us -> 19.7 us  [body(): back = lax.all_to_all(back, HEAD, split_axis=0, concat_axis=0, tiled=True)]
    pallas_call x1, Pallas kernels: 10.6 us -> 11.8 us  [head_target(): pl.pallas_call(functools.partial(target_kernel, skip), in_specs=[SCALARS,...]
    unnamed x12 -> x16, local copies, waits for them, and re-layouts: 3.14 us -> 2.47 us
  transfers between devices with their start and end apart: 19 -> 22, of which waited for: 11 -> 12; matrix products, arithmetic and copies ran while one was open for 2% -> 2% of each run, Pallas kernels for 13% -> 5%
where the time goes in v2:
time: 116 us; the launch traced here: 115 us
  starting transfers between devices  35.8 us (31%)
  waiting for transfers between devices  31.2 us (27%)
  Pallas kernels  20.2 us (17%)
  blocking collectives  19.7 us (17%)
  local copies, waits for them, and re-layouts  4.38 us (4%)
  other arithmetic  3.12 us (3%)
    ppermute x15, waiting for transfers between devices, take(): return lax.ppermute(a, axis, [((i + shift) % n, i) for i in range(n)])  23.6 us
    all_to_all x1, blocking collectives, body(): back = lax.all_to_all(back, HEAD, split_axis=0, concat_axis=0, tiled=True)  19.7 us
    ppermute x15, starting transfers between devices, take(): return lax.ppermute(a, axis, [((i + shift) % n, i) for i in range(n)])  16.5 us
    ppermute x6, starting transfers between devices, take_z(): lax.ppermute(a, ('z', 'w'), [(place(i + shift), place(i)) for i in range(...  12 us
    pallas_call x1, Pallas kernels, head_target(): pl.pallas_call(functools.partial(target_kernel, skip), in_specs=[SCALARS,...  11.8 us
    all_to_all x1, starting transfers between devices, gather_keys(): got = lax.all_to_all(sent, HEAD, split_axis=0, concat_axis=0, tiled=True)  7.35 us
    all_to_all x1, waiting for transfers between devices, gather_keys(): got = lax.all_to_all(sent, HEAD, split_axis=0, concat_axis=0, tiled=True)  3.81 us
    ppermute x6, waiting for transfers between devices, take_z(): lax.ppermute(a, ('z', 'w'), [(place(i + shift), place(i)) for i in range(...  3.77 us
  transfers between devices with their start and end apart: 22, of which 12 were waited for; matrix products, arithmetic and copies ran while one was open for 2% of the time, Pallas kernels for 5%

profile of v2, /device:TPU:64, one launch (start us, length us, event | category | flops | bytes accessed | tf_op | source)
XLA Modules:
  0.0 115.3 jit_solution(15598033047803982389)
XLA Ops:
  1.9 1.9 %collective-permute-start.1 = (bf16[64,768]{1,0:T(8,128)(2,1)S(1)}, bf16[64,768]{1,0:T(8,128)(2,1)S(1)}, u32[]{:S(2)}, u32[]{:S(2)}) collective-permute-start(bf16[64,768]{1,0:T(8,128)(2,1)S(1)} %pad_maximum_fusion.2), channel_id=1, source_target_pairs={{49,0},{0,16},{16,32},{32,48},{48,1},{1,17},{17,33},{33,49},{51,2}... | collective-permute-start | bytes 294920 | tf_op jit(solution)/shard_map/ppermute | solution.py:277
  3.9 3.5 %collective-permute-start.2 = (bf16[64,768]{1,0:T(8,128)(2,1)S(1)}, bf16[64,768]{1,0:T(8,128)(2,1)S(1)}, u32[]{:S(2)}, u32[]{:S(2)}) collective-permute-start(bf16[64,768]{1,0:T(8,128)(2,1)S(1)} %pad_maximum_fusion.2), channel_id=1, source_target_pairs={{32,0},{48,16},{1,32},{17,48},{33,1},{49,17},{0,33},{16,49},{34,2}... | collective-permute-start | bytes 294920 | tf_op jit(solution)/shard_map/ppermute | solution.py:277
  8.8 1.7 %pack_index.1 = bf16[8,144,128]{2,1,0:T(8,128)(2,1)} custom-call(bf16[8,128,128]{2,1,0:T(8,128)(2,1)} %bitcast.43, f32[8,128]{1,0:T(8,128)} %reshape.72.w_ref), custom_call_target="tpu_custom_call" | custom-call | tf_op jit(solution)/shard_map/pack_index/pallas_call | solution.py:127
  10.5 2.1 %collective-permute-done.2 = bf16[64,768]{1,0:T(8,128)(2,1)S(1)} collective-permute-done((bf16[64,768]{1,0:T(8,128)(2,1)S(1)}, bf16[64,768]{1,0:T(8,128)(2,1)S(1)}, u32[]{:S(2)}, u32[]{:S(2)}) %collective-permute-start.2) | collective-permute-done | bytes 98336 | tf_op jit(solution)/shard_map/ppermute | solution.py:277
  13.6 3.3 %collective-permute-start.3 = (bf16[256,768]{1,0:T(8,128)(2,1)S(1)}, bf16[256,768]{1,0:T(8,128)(2,1)}, u32[]{:S(2)}, u32[]{:S(2)}) collective-permute-start(bf16[256,768]{1,0:T(8,128)(2,1)S(1)} %pad_maximum_fusion.1.refs_0_), channel_id=1, source_target_pairs={{128,0},{192,64},{0,128},{64,192},{129,1},{193,65},{1,129},{65,193... | collective-permute-start | bytes 1179656 | tf_op jit(solution)/shard_map/ppermute | solution.py:272
  18.9 7.3 %all-to-all-start = ((bf16[8,144,128]{2,1,0:T(8,128)(2,1)}), bf16[8,144,128]{2,1,0:T(8,128)(2,1)S(1)}, u32[]{:S(2)}, u32[]{:S(2)}) async-start(bf16[8,144,128]{2,1,0:T(8,128)(2,1)} %pack_index.1), calls=%async_computation | async-start | bytes 589824 | tf_op jit(solution)/shard_map/all_to_all | solution.py:286
  27.4 5.6 %collective-permute-done.5.refs_1_ = bf16[256,768]{1,0:T(8,128)(2,1)} collective-permute-done((bf16[256,768]{1,0:T(8,128)(2,1)S(1)}, bf16[256,768]{1,0:T(8,128)(2,1)}, u32[]{:S(2)}, u32[]{:S(2)}) %collective-permute-start.5) | collective-permute-done | bytes 393248 | tf_op jit(solution)/shard_map/ppermute | solution.py:272
  33.9 3.8 %all-to-all-done.got_ref = bf16[8,144,128]{2,1,0:T(8,128)(2,1)S(1)} async-done(((bf16[8,144,128]{2,1,0:T(8,128)(2,1)}), bf16[8,144,128]{2,1,0:T(8,128)(2,1)S(1)}, u32[]{:S(2)}, u32[]{:S(2)}) %all-to-all-start) | async-done | bytes 294944 | tf_op jit(solution)/shard_map/all_to_all | solution.py:286
  38.7 11.8 %head_target.1 = (bf16[2,16,2048]{2,1,0:T(8,128)(2,1)S(1)}, bf16[2,16,2048]{2,1,0:T(8,128)(2,1)}, bf16[2,16,2048]{2,1,0:T(8,128)(2,1)S(1)}, bf16[2,16,2048]{2,1,0:T(8,128)(2,1)}, bf16[2048,128]{1,0:T(8,128)(2,1)S(1)}) custom-call(s32[32]{0:T(128)S(1)} %add_multiply_fusion.base_ref, s32[8]{0:T(128)S(1)} %stack.35.offset_ref, ...), custom_call_target="tpu_custom_call" | custom-call | tf_op jit(solution)/shard_map/head_target/pallas_call | solution.py:94
  51.5 2.4 %collective-permute-start.11 = (bf16[2,16,2048]{2,1,0:T(8,128)(2,1)}, bf16[2,16,2048]{2,1,0:T(8,128)(2,1)S(1)}, u32[]{:S(2)}, u32[]{:S(2)}) collective-permute-start(bf16[2,16,2048]{2,1,0:T(8,128)(2,1)} %get-tuple-element.38), channel_id=1, source_target_pairs={{2,0},{4,2},{6,4},{0,6},{3,1},{5,3},{7,5},{1,7},{10,8},{12,10},{14... | collective-permute-start | bytes 393224 | tf_op jit(solution)/shard_map/ppermute | solution.py:272
  55.6 2.8 %collective-permute-done.10 = bf16[2,16,2048]{2,1,0:T(8,128)(2,1)S(1)} collective-permute-done((bf16[2,16,2048]{2,1,0:T(8,128)(2,1)}, bf16[2,16,2048]{2,1,0:T(8,128)(2,1)S(1)}, u32[]{:S(2)}, u32[]{:S(2)}) %collective-permute-start.10) | collective-permute-done | bytes 131104 | tf_op jit(solution)/shard_map/ppermute | solution.py:272
  58.4 2.0 %collective-permute-done.12 = bf16[2,16,2048]{2,1,0:T(8,128)(2,1)S(1)} collective-permute-done((bf16[2,16,2048]{2,1,0:T(8,128)(2,1)S(1)}, bf16[2,16,2048]{2,1,0:T(8,128)(2,1)S(1)}, u32[]{:S(2)}, u32[]{:S(2)}) %collective-permute-start.12) | collective-permute-done | bytes 131104 | tf_op jit(solution)/shard_map/ppermute | solution.py:272
  60.4 3.2 %collective-permute-start.13 = (bf16[16,2048]{1,0:T(8,128)(2,1)S(1)}, bf16[16,2048]{1,0:T(8,128)(2,1)S(1)}, u32[]{:S(2)}, u32[]{:S(2)}) collective-permute-start(bf16[16,2048]{1,0:T(8,128)(2,1)S(1)} %fusion.4), channel_id=1, source_target_pairs={{1,0},{0,1},{3,2},{2,3},{5,4},{4,5},{7,6},{6,7},{9,8},{8,9},{11,10... | collective-permute-start | bytes 196616 | tf_op jit(solution)/shard_map/ppermute | solution.py:272
  63.6 5.3 %collective-permute-done.13.part_ref = bf16[16,2048]{1,0:T(8,128)(2,1)S(1)} collective-permute-done((bf16[16,2048]{1,0:T(8,128)(2,1)S(1)}, bf16[16,2048]{1,0:T(8,128)(2,1)S(1)}, u32[]{:S(2)}, u32[]{:S(2)}) %collective-permute-start.13) | collective-permute-done | bytes 65568 | tf_op jit(solution)/shard_map/ppermute | solution.py:272
  68.9 2.5 %key_backward.1 = f32[32,64,128]{2,1,0:T(8,128)S(1)} custom-call(s32[32]{0:T(128)S(1)} %copy-done.4, bf16[8,144,128]{2,1,0:T(8,128)(2,1)S(1)} %all-to-all-done.got_ref, bf16[2048,128]{1,0:T(8,128)(2,1)S(1)} %get-tuple-element.35.k_ref, f32[16,2048]{1,0:T(8,128)S(1)} %index_prob.1.prob_ref, f32[16,2048]{1,0:T(8,128)S(1)} %slice_bitcast_fusion.near_ref, ...), custom_call_target="tpu_custom_call" | custom-call | tf_op jit(solution)/shard_map/key_backward/pallas_call | solution.py:240
  71.6 1.9 %collective-permute-done.14 = f32[16,64,128]{2,1,0:T(8,128)S(1)} collective-permute-done((f32[16,64,128]{2,1,0:T(8,128)S(1)}, f32[16,64,128]{2,1,0:T(8,128)S(1)}, u32[]{:S(2)}, u32[]{:S(2)}) %collective-permute-start.14) | collective-permute-done | bytes 524320 | tf_op jit(solution)/shard_map/ppermute | solution.py:272
  74.4 2.5 %collective-permute-start.16 = (bf16[4,64,128]{2,1,0:T(8,128)(2,1)S(1)}, bf16[4,64,128]{2,1,0:T(8,128)(2,1)S(1)}, u32[]{:S(2)}, u32[]{:S(2)}) collective-permute-start(bf16[4,64,128]{2,1,0:T(8,128)(2,1)S(1)} %get-tuple-element.57), channel_id=1, source_target_pairs={{64,0},{128,64},{192,128},{0,192},{65,1},{129,65},{193,129},{1,193... | collective-permute-start | bytes 196616 | tf_op jit(solution)/shard_map/ppermute | solution.py:272
  79.4 3.3 %collective-permute-done.17 = bf16[4,64,128]{2,1,0:T(8,128)(2,1)S(1)} collective-permute-done((bf16[4,64,128]{2,1,0:T(8,128)(2,1)S(1)}, bf16[4,64,128]{2,1,0:T(8,128)(2,1)S(1)}, u32[]{:S(2)}, u32[]{:S(2)}) %collective-permute-start.17) | collective-permute-done | bytes 65568 | tf_op jit(solution)/shard_map/ppermute | solution.py:272
  82.7 3.1 %collective-permute-start.18 = (bf16[64,128]{1,0:T(8,128)(2,1)S(1)}, bf16[64,128]{1,0:T(8,128)(2,1)S(1)}, u32[]{:S(2)}, u32[]{:S(2)}) collective-permute-start(bf16[64,128]{1,0:T(8,128)(2,1)S(1)} %get-tuple-element.61), channel_id=1, source_target_pairs={{49,0},{0,16},{16,32},{32,48},{48,1},{1,17},{17,33},{33,49},{51,2}... | collective-permute-start | bytes 49160 | tf_op jit(solution)/shard_map/ppermute | solution.py:277
  85.9 1.7 %collective-permute-start.19 = (bf16[64,128]{1,0:T(8,128)(2,1)S(1)}, bf16[64,128]{1,0:T(8,128)(2,1)S(1)}, u32[]{:S(2)}, u32[]{:S(2)}) collective-permute-start(bf16[64,128]{1,0:T(8,128)(2,1)S(1)} %get-tuple-element.60), channel_id=1, source_target_pairs={{16,0},{32,16},{48,32},{1,48},{17,1},{33,17},{49,33},{0,49},{18,2}... | collective-permute-start | bytes 49160 | tf_op jit(solution)/shard_map/ppermute | solution.py:277
  87.5 1.6 %collective-permute-start.20 = (bf16[64,128]{1,0:T(8,128)(2,1)S(1)}, bf16[64,128]{1,0:T(8,128)(2,1)S(1)}, u32[]{:S(2)}, u32[]{:S(2)}) collective-permute-start(bf16[64,128]{1,0:T(8,128)(2,1)S(1)} %get-tuple-element.59), channel_id=1, source_target_pairs={{32,0},{48,16},{1,32},{17,48},{33,1},{49,17},{0,33},{16,49},{34,2}... | collective-permute-start | bytes 49160 | tf_op jit(solution)/shard_map/ppermute | solution.py:277
  89.2 2.5 %query_backward.1 = bf16[8,144,128]{2,1,0:T(8,128)(2,1)S(1)} custom-call(bf16[8,144,128]{2,1,0:T(8,128)(2,1)S(1)} %all-to-all-done.got_ref, bf16[2048,128]{1,0:T(8,128)(2,1)S(1)} %get-tuple-element.35.k_ref, f32[16,2048]{1,0:T(8,128)S(1)} %index_prob.1.prob_ref, f32[16,2048]{1,0:T(8,128)S(1)} %slice_bitcast_fusion.near_ref, ...), custom_call_target="tpu_custom_call" | custom-call | tf_op jit(solution)/shard_map/query_backward/pallas_call | solution.py:255
  91.7 1.7 %collective-permute-done.20 = bf16[64,128]{1,0:T(8,128)(2,1)S(1)} collective-permute-done((bf16[64,128]{1,0:T(8,128)(2,1)S(1)}, bf16[64,128]{1,0:T(8,128)(2,1)S(1)}, u32[]{:S(2)}, u32[]{:S(2)}) %collective-permute-start.20) | collective-permute-done | bytes 16416 | tf_op jit(solution)/shard_map/ppermute | solution.py:277
  93.5 19.7 %all_to_all.10 = bf16[8,208,128]{2,1,0:T(8,128)(2,1)S(1)} all-to-all(bf16[8,208,128]{2,1,0:T(8,128)(2,1)S(1)} %pad_maximum_fusion), channel_id=1, replica_groups=mesh['y'=4,'z'=4,'c'=2,'x'=4,'w'=2] {'x','w'}, dimensions={0} | all-to-all | bytes 851968 | tf_op jit(solution)/shard_map/all_to_all | solution.py:347
  (69 shorter events, 17.2 us)
Async XLA Ops:
  0.7 32.9 %copy-start.3 = (s32[128]{0:T(128)S(1)}, s32[128]{0:T(128)}, u32[]{:S(2)}) copy-start(s32[128]{0:T(128)} %param.13) | copy-start | bytes 1540
  0.7 37.0 %copy-start = (bf16[128,16,576]{0,2,1:T(8,128)(2,1)S(1)}, bf16[128,16,576]{0,2,1:T(8,128)(2,1)}, u32[]{:S(2)}) copy-start(bf16[128,16,576]{0,2,1:T(8,128)(2,1)} %param.8) | copy-start | bytes 7077892
  1.8 8.7 %collective-permute-start = (bf16[64,768]{1,0:T(8,128)(2,1)S(1)}, bf16[64,768]{1,0:T(8,128)(2,1)S(1)}, u32[]{:S(2)}, u32[]{:S(2)}) collective-permute-start(bf16[64,768]{1,0:T(8,128)(2,1)S(1)} %pad_maximum_fusion.2), channel_id=1, source_target_pairs={{16,0},{32,16},{48,32},{1,48},{17,1},{33,17},{49,33},{0,49},{18,2}... | collective-permute-start | bytes 294920 | tf_op jit(solution)/shard_map/ppermute | solution.py:277
  1.9 8.6 %collective-permute-start.1 = (bf16[64,768]{1,0:T(8,128)(2,1)S(1)}, bf16[64,768]{1,0:T(8,128)(2,1)S(1)}, u32[]{:S(2)}, u32[]{:S(2)}) collective-permute-start(bf16[64,768]{1,0:T(8,128)(2,1)S(1)} %pad_maximum_fusion.2), channel_id=1, source_target_pairs={{49,0},{0,16},{16,32},{32,48},{48,1},{1,17},{17,33},{33,49},{51,2}... | collective-permute-start | bytes 294920 | tf_op jit(solution)/shard_map/ppermute | solution.py:277
  3.9 8.7 %collective-permute-start.2 = (bf16[64,768]{1,0:T(8,128)(2,1)S(1)}, bf16[64,768]{1,0:T(8,128)(2,1)S(1)}, u32[]{:S(2)}, u32[]{:S(2)}) collective-permute-start(bf16[64,768]{1,0:T(8,128)(2,1)S(1)} %pad_maximum_fusion.2), channel_id=1, source_target_pairs={{32,0},{48,16},{1,32},{17,48},{33,1},{49,17},{0,33},{16,49},{34,2}... | collective-permute-start | bytes 294920 | tf_op jit(solution)/shard_map/ppermute | solution.py:277
  13.6 13.8 %collective-permute-start.3 = (bf16[256,768]{1,0:T(8,128)(2,1)S(1)}, bf16[256,768]{1,0:T(8,128)(2,1)}, u32[]{:S(2)}, u32[]{:S(2)}) collective-permute-start(bf16[256,768]{1,0:T(8,128)(2,1)S(1)} %pad_maximum_fusion.1.refs_0_), channel_id=1, source_target_pairs={{128,0},{192,64},{0,128},{64,192},{129,1},{193,65},{1,129},{65,193... | collective-permute-start | bytes 1179656 | tf_op jit(solution)/shard_map/ppermute | solution.py:272
  16.9 16.1 %collective-permute-start.5 = (bf16[256,768]{1,0:T(8,128)(2,1)S(1)}, bf16[256,768]{1,0:T(8,128)(2,1)}, u32[]{:S(2)}, u32[]{:S(2)}) collective-permute-start(bf16[256,768]{1,0:T(8,128)(2,1)S(1)} %pad_maximum_fusion.1.refs_0_), channel_id=1, source_target_pairs={{64,0},{128,64},{192,128},{0,192},{65,1},{129,65},{193,129},{1,193... | collective-permute-start | bytes 1179656 | tf_op jit(solution)/shard_map/ppermute | solution.py:272
  17.9 15.1 %collective-permute-start.6 = (bf16[256,768]{1,0:T(8,128)(2,1)S(1)}, bf16[256,768]{1,0:T(8,128)(2,1)}, u32[]{:S(2)}, u32[]{:S(2)}) collective-permute-start(bf16[256,768]{1,0:T(8,128)(2,1)S(1)} %pad_maximum_fusion.1.refs_0_), channel_id=1, source_target_pairs={{192,0},{0,64},{64,128},{128,192},{193,1},{1,65},{65,129},{129,193... | collective-permute-start | bytes 1179656 | tf_op jit(solution)/shard_map/ppermute | solution.py:272
  18.9 18.8 %all-to-all-start = ((bf16[8,144,128]{2,1,0:T(8,128)(2,1)}), bf16[8,144,128]{2,1,0:T(8,128)(2,1)S(1)}, u32[]{:S(2)}, u32[]{:S(2)}) async-start(bf16[8,144,128]{2,1,0:T(8,128)(2,1)} %pack_index.1), calls=%async_computation | async-start | bytes 589824 | tf_op jit(solution)/shard_map/all_to_all | solution.py:286
  26.3 11.3 %collective-permute-start.7 = (bf16[256,768]{1,0:T(8,128)(2,1)S(1)}, bf16[256,768]{1,0:T(8,128)(2,1)}, u32[]{:S(2)}, u32[]{:S(2)}) collective-permute-start(bf16[256,768]{1,0:T(8,128)(2,1)S(1)} %pad_maximum_fusion.1.refs_0_), channel_id=1, source_target_pairs={{8,0},{0,8},{9,1},{1,9},{10,2},{2,10},{11,3},{3,11},{12,4},{4,12},... | collective-permute-start | bytes 1179656 | tf_op jit(solution)/shard_map/ppermute | solution.py:272
  27.4 10.3 %collective-permute-start.4 = (bf16[256,768]{1,0:T(8,128)(2,1)}, bf16[256,768]{1,0:T(8,128)(2,1)}, u32[]{:S(2)}, u32[]{:S(2)}) collective-permute-start(bf16[256,768]{1,0:T(8,128)(2,1)} %collective-permute-done.3.refs_3_), channel_id=1, source_target_pairs={{8,0},{0,8},{9,1},{1,9},{10,2},{2,10},{11,3},{3,11},{12,4},{4,12},... | collective-permute-start | bytes 1179656 | tf_op jit(solution)/shard_map/ppermute | solution.py:272
  33.0 4.7 %collective-permute-start.8 = (bf16[256,768]{1,0:T(8,128)(2,1)}, bf16[256,768]{1,0:T(8,128)(2,1)}, u32[]{:S(2)}, u32[]{:S(2)}) collective-permute-start(bf16[256,768]{1,0:T(8,128)(2,1)} %collective-permute-done.5.refs_1_), channel_id=1, source_target_pairs={{8,0},{0,8},{9,1},{1,9},{10,2},{2,10},{11,3},{3,11},{12,4},{4,12},... | collective-permute-start | bytes 1179656 | tf_op jit(solution)/shard_map/ppermute | solution.py:272
  33.0 4.7 %collective-permute-start.9 = (bf16[256,768]{1,0:T(8,128)(2,1)}, bf16[256,768]{1,0:T(8,128)(2,1)}, u32[]{:S(2)}, u32[]{:S(2)}) collective-permute-start(bf16[256,768]{1,0:T(8,128)(2,1)} %collective-permute-done.6.refs_2_), channel_id=1, source_target_pairs={{8,0},{0,8},{9,1},{1,9},{10,2},{2,10},{11,3},{3,11},{12,4},{4,12},... | collective-permute-start | bytes 1179656 | tf_op jit(solution)/shard_map/ppermute | solution.py:272
  50.6 7.8 %collective-permute-start.10 = (bf16[2,16,2048]{2,1,0:T(8,128)(2,1)}, bf16[2,16,2048]{2,1,0:T(8,128)(2,1)S(1)}, u32[]{:S(2)}, u32[]{:S(2)}) collective-permute-start(bf16[2,16,2048]{2,1,0:T(8,128)(2,1)} %get-tuple-element.37), channel_id=1, source_target_pairs={{6,0},{0,2},{2,4},{4,6},{7,1},{1,3},{3,5},{5,7},{14,8},{8,10},{10,... | collective-permute-start | bytes 393224 | tf_op jit(solution)/shard_map/ppermute | solution.py:272
  51.5 6.9 %collective-permute-start.11 = (bf16[2,16,2048]{2,1,0:T(8,128)(2,1)}, bf16[2,16,2048]{2,1,0:T(8,128)(2,1)S(1)}, u32[]{:S(2)}, u32[]{:S(2)}) collective-permute-start(bf16[2,16,2048]{2,1,0:T(8,128)(2,1)} %get-tuple-element.38), channel_id=1, source_target_pairs={{2,0},{4,2},{6,4},{0,6},{3,1},{5,3},{7,5},{1,7},{10,8},{12,10},{14... | collective-permute-start | bytes 393224 | tf_op jit(solution)/shard_map/ppermute | solution.py:272
  53.9 6.5 %collective-permute-start.12 = (bf16[2,16,2048]{2,1,0:T(8,128)(2,1)S(1)}, bf16[2,16,2048]{2,1,0:T(8,128)(2,1)S(1)}, u32[]{:S(2)}, u32[]{:S(2)}) collective-permute-start(bf16[2,16,2048]{2,1,0:T(8,128)(2,1)S(1)} %get-tuple-element.39), channel_id=1, source_target_pairs={{4,0},{6,2},{0,4},{2,6},{5,1},{7,3},{1,5},{3,7},{12,8},{14,10},{8,... | collective-permute-start | bytes 393224 | tf_op jit(solution)/shard_map/ppermute | solution.py:272
  60.4 8.5 %collective-permute-start.13 = (bf16[16,2048]{1,0:T(8,128)(2,1)S(1)}, bf16[16,2048]{1,0:T(8,128)(2,1)S(1)}, u32[]{:S(2)}, u32[]{:S(2)}) collective-permute-start(bf16[16,2048]{1,0:T(8,128)(2,1)S(1)} %fusion.4), channel_id=1, source_target_pairs={{1,0},{0,1},{3,2},{2,3},{5,4},{4,5},{7,6},{6,7},{9,8},{8,9},{11,10... | collective-permute-start | bytes 196616 | tf_op jit(solution)/shard_map/ppermute | solution.py:272
  71.5 2.0 %collective-permute-start.14 = (f32[16,64,128]{2,1,0:T(8,128)S(1)}, f32[16,64,128]{2,1,0:T(8,128)S(1)}, u32[]{:S(2)}, u32[]{:S(2)}) collective-permute-start(f32[16,64,128]{2,1,0:T(8,128)S(1)} %slice.64), channel_id=1, source_target_pairs={{8,0},{0,8},{9,1},{1,9},{10,2},{2,10},{11,3},{3,11},{12,4},{4,12},... | collective-permute-start | bytes 1572872 | tf_op jit(solution)/shard_map/ppermute | solution.py:272
  73.6 5.6 %collective-permute-start.15 = (bf16[4,64,128]{2,1,0:T(8,128)(2,1)S(1)}, bf16[4,64,128]{2,1,0:T(8,128)(2,1)S(1)}, u32[]{:S(2)}, u32[]{:S(2)}) collective-permute-start(bf16[4,64,128]{2,1,0:T(8,128)(2,1)S(1)} %get-tuple-element.58), channel_id=1, source_target_pairs={{192,0},{0,64},{64,128},{128,192},{193,1},{1,65},{65,129},{129,193... | collective-permute-start | bytes 196616 | tf_op jit(solution)/shard_map/ppermute | solution.py:272
  74.4 5.0 %collective-permute-start.16 = (bf16[4,64,128]{2,1,0:T(8,128)(2,1)S(1)}, bf16[4,64,128]{2,1,0:T(8,128)(2,1)S(1)}, u32[]{:S(2)}, u32[]{:S(2)}) collective-permute-start(bf16[4,64,128]{2,1,0:T(8,128)(2,1)S(1)} %get-tuple-element.57), channel_id=1, source_target_pairs={{64,0},{128,64},{192,128},{0,192},{65,1},{129,65},{193,129},{1,193... | collective-permute-start | bytes 196616 | tf_op jit(solution)/shard_map/ppermute | solution.py:272
  76.9 5.8 %collective-permute-start.17 = (bf16[4,64,128]{2,1,0:T(8,128)(2,1)S(1)}, bf16[4,64,128]{2,1,0:T(8,128)(2,1)S(1)}, u32[]{:S(2)}, u32[]{:S(2)}) collective-permute-start(bf16[4,64,128]{2,1,0:T(8,128)(2,1)S(1)} %get-tuple-element.56), channel_id=1, source_target_pairs={{128,0},{192,64},{0,128},{64,192},{129,1},{193,65},{1,129},{65,193... | collective-permute-start | bytes 196616 | tf_op jit(solution)/shard_map/ppermute | solution.py:272
  82.7 9.0 %collective-permute-start.18 = (bf16[64,128]{1,0:T(8,128)(2,1)S(1)}, bf16[64,128]{1,0:T(8,128)(2,1)S(1)}, u32[]{:S(2)}, u32[]{:S(2)}) collective-permute-start(bf16[64,128]{1,0:T(8,128)(2,1)S(1)} %get-tuple-element.61), channel_id=1, source_target_pairs={{49,0},{0,16},{16,32},{32,48},{48,1},{1,17},{17,33},{33,49},{51,2}... | collective-permute-start | bytes 49160 | tf_op jit(solution)/shard_map/ppermute | solution.py:277
  85.9 5.9 %collective-permute-start.19 = (bf16[64,128]{1,0:T(8,128)(2,1)S(1)}, bf16[64,128]{1,0:T(8,128)(2,1)S(1)}, u32[]{:S(2)}, u32[]{:S(2)}) collective-permute-start(bf16[64,128]{1,0:T(8,128)(2,1)S(1)} %get-tuple-element.60), channel_id=1, source_target_pairs={{16,0},{32,16},{48,32},{1,48},{17,1},{33,17},{49,33},{0,49},{18,2}... | collective-permute-start | bytes 49160 | tf_op jit(solution)/shard_map/ppermute | solution.py:277
  87.5 5.9 %collective-permute-start.20 = (bf16[64,128]{1,0:T(8,128)(2,1)S(1)}, bf16[64,128]{1,0:T(8,128)(2,1)S(1)}, u32[]{:S(2)}, u32[]{:S(2)}) collective-permute-start(bf16[64,128]{1,0:T(8,128)(2,1)S(1)} %get-tuple-element.59), channel_id=1, source_target_pairs={{32,0},{48,16},{1,32},{17,48},{33,1},{49,17},{0,33},{16,49},{34,2}... | collective-permute-start | bytes 49160 | tf_op jit(solution)/shard_map/ppermute | solution.py:277
  (5 other events, 106.5 us)

commit v3 on v2

--- a/solution.py
+++ b/solution.py
@@ -19,13 +19,12 @@
 f32 = jnp.float32
 bf16 = jnp.bfloat16
 HELD = pl.BlockSpec(memory_space=pltpu.VMEM)
-ANYWHERE = pl.BlockSpec(memory_space=pl.ANY)
 SCALARS = pl.BlockSpec(memory_space=pltpu.SMEM)
 
 
 def target_kernel(skip, base_ref, offset_ref, q_ref, vis_ref, *refs):
-    index_ref, bias_ref, s_ref, p_ref, sum_ref, turn_ref, out_sem = refs[-7:]
-    blocks, outs = refs[:-11], refs[-11:-7]
+    index_ref, bias_ref, s_ref, p_ref, sum_ref, turn_ref = refs[-6:]
+    blocks, outs = refs[:-10], refs[-10:-6]
     heads, depth, rows = q_ref.shape
     key_count = bias_ref.shape[0]
     unit = key_count // base_ref.shape[0]
@@ -72,16 +71,10 @@
             shares[step - 1] = 1.0 / (total * MLA_HEADS)
     for start in range(0, key_count, rows):
         turn_ref[:, start : start + rows] = sum_ref[start : start + rows].T.astype(bf16)
-    stores = []
     for i, out in enumerate(outs):
         for j in range(out.shape[0]):
-            number = i * out.shape[0] + j
-            start = pl.multiple_of(offset_ref[number], out.shape[1])
-            source = turn_ref.at[pl.ds(start, out.shape[1])]
-            stores.append(pltpu.make_async_copy(source, out.at[j], out_sem.at[number]))
-            stores[-1].start()
-    for store in stores:
-        store.wait()
+            start = pl.multiple_of(offset_ref[i * out.shape[0] + j], out.shape[1])
+            out[j] = turn_ref[pl.ds(start, out.shape[1])]
 
 
 def head_target(queries, blocks, visible, base, offsets, skip):
@@ -94,7 +87,7 @@
     return pl.pallas_call(
         functools.partial(target_kernel, skip),
         in_specs=[SCALARS, SCALARS] + [HELD] * (2 + len(blocks)),
-        out_specs=[ANYWHERE] * 4 + [HELD],
+        out_specs=[HELD] * 5,
         out_shape=outs + [jax.ShapeDtypeStruct((key_count, skip), bf16)],
         scratch_shapes=[
             pltpu.VMEM((key_count, row_count), f32),
@@ -102,7 +95,6 @@
             pltpu.VMEM((2, key_count, 2 * row_count), f32),
             pltpu.VMEM((key_count, row_count), f32),
             pltpu.VMEM((row_count, key_count), bf16),
-            pltpu.SemaphoreType.DMA((offsets.shape[0],)),
         ],
         compiler_params=pltpu.CompilerParams(vmem_limit_bytes=24 << 20),
         name="head_target",

time: 116 us -> 115 us (level)
  no operation moved by 1% of the time
where the time goes in v3:
time: 115 us
  starting transfers between devices  35.7 us (31%)
  waiting for transfers between devices  31.2 us (27%)
  Pallas kernels  19.8 us (17%)
  blocking collectives  19.7 us (17%)
  local copies, waits for them, and re-layouts  4.38 us (4%)
  other arithmetic  3.12 us (3%)
    ppermute x15, waiting for transfers between devices, take(): return lax.ppermute(a, axis, [((i + shift) % n, i) for i in range(n)])  23.6 us
    all_to_all x1, blocking collectives, body(): back = lax.all_to_all(back, HEAD, split_axis=0, concat_axis=0, tiled=True)  19.7 us
    ppermute x15, starting transfers between devices, take(): return lax.ppermute(a, axis, [((i + shift) % n, i) for i in range(n)])  16.4 us
    ppermute x6, starting transfers between devices, take_z(): lax.ppermute(a, ('z', 'w'), [(place(i + shift), place(i)) for i in range(...  12 us
    pallas_call x1, Pallas kernels, head_target(): pl.pallas_call(functools.partial(target_kernel, skip), in_specs=[SCALARS,...  11.5 us
    all_to_all x1, starting transfers between devices, gather_keys(): got = lax.all_to_all(sent, HEAD, split_axis=0, concat_axis=0, tiled=True)  7.35 us
    all_to_all x1, waiting for transfers between devices, gather_keys(): got = lax.all_to_all(sent, HEAD, split_axis=0, concat_axis=0, tiled=True)  3.81 us
    ppermute x6, waiting for transfers between devices, take_z(): lax.ppermute(a, ('z', 'w'), [(place(i + shift), place(i)) for i in range(...  3.77 us
  transfers between devices with their start and end apart: 22, of which 12 were waited for; matrix products, arithmetic and copies ran while one was open for 2% of the time, Pallas kernels for 5%

profile of v3, /device:TPU:64, one launch (start us, length us, event | category | flops | bytes accessed | tf_op | source)
XLA Modules:
  0.0 114.8 jit_solution(3631834373100515794)
XLA Ops:
  1.9 1.9 %collective-permute-start.1 = (bf16[64,768]{1,0:T(8,128)(2,1)S(1)}, bf16[64,768]{1,0:T(8,128)(2,1)S(1)}, u32[]{:S(2)}, u32[]{:S(2)}) collective-permute-start(bf16[64,768]{1,0:T(8,128)(2,1)S(1)} %pad_maximum_fusion.2), channel_id=1, source_target_pairs={{49,0},{0,16},{16,32},{32,48},{48,1},{1,17},{17,33},{33,49},{51,2}... | collective-permute-start | bytes 294920 | tf_op jit(solution)/shard_map/ppermute | solution.py:269
  3.9 3.5 %collective-permute-start.2 = (bf16[64,768]{1,0:T(8,128)(2,1)S(1)}, bf16[64,768]{1,0:T(8,128)(2,1)S(1)}, u32[]{:S(2)}, u32[]{:S(2)}) collective-permute-start(bf16[64,768]{1,0:T(8,128)(2,1)S(1)} %pad_maximum_fusion.2), channel_id=1, source_target_pairs={{32,0},{48,16},{1,32},{17,48},{33,1},{49,17},{0,33},{16,49},{34,2}... | collective-permute-start | bytes 294920 | tf_op jit(solution)/shard_map/ppermute | solution.py:269
  8.8 1.7 %pack_index.1 = bf16[8,144,128]{2,1,0:T(8,128)(2,1)} custom-call(bf16[8,128,128]{2,1,0:T(8,128)(2,1)} %bitcast.43, f32[8,128]{1,0:T(8,128)} %reshape.72.w_ref), custom_call_target="tpu_custom_call" | custom-call | tf_op jit(solution)/shard_map/pack_index/pallas_call | solution.py:119
  10.5 2.1 %collective-permute-done.2 = bf16[64,768]{1,0:T(8,128)(2,1)S(1)} collective-permute-done((bf16[64,768]{1,0:T(8,128)(2,1)S(1)}, bf16[64,768]{1,0:T(8,128)(2,1)S(1)}, u32[]{:S(2)}, u32[]{:S(2)}) %collective-permute-start.2) | collective-permute-done | bytes 98336 | tf_op jit(solution)/shard_map/ppermute | solution.py:269
  13.6 3.3 %collective-permute-start.3 = (bf16[256,768]{1,0:T(8,128)(2,1)S(1)}, bf16[256,768]{1,0:T(8,128)(2,1)}, u32[]{:S(2)}, u32[]{:S(2)}) collective-permute-start(bf16[256,768]{1,0:T(8,128)(2,1)S(1)} %pad_maximum_fusion.1.refs_0_), channel_id=1, source_target_pairs={{128,0},{192,64},{0,128},{64,192},{129,1},{193,65},{1,129},{65,193... | collective-permute-start | bytes 1179656 | tf_op jit(solution)/shard_map/ppermute | solution.py:264
  18.9 7.3 %all-to-all-start = ((bf16[8,144,128]{2,1,0:T(8,128)(2,1)}), bf16[8,144,128]{2,1,0:T(8,128)(2,1)S(1)}, u32[]{:S(2)}, u32[]{:S(2)}) async-start(bf16[8,144,128]{2,1,0:T(8,128)(2,1)} %pack_index.1), calls=%async_computation | async-start | bytes 589824 | tf_op jit(solution)/shard_map/all_to_all | solution.py:278
  27.4 5.6 %collective-permute-done.5.refs_1_ = bf16[256,768]{1,0:T(8,128)(2,1)} collective-permute-done((bf16[256,768]{1,0:T(8,128)(2,1)S(1)}, bf16[256,768]{1,0:T(8,128)(2,1)}, u32[]{:S(2)}, u32[]{:S(2)}) %collective-permute-start.5) | collective-permute-done | bytes 393248 | tf_op jit(solution)/shard_map/ppermute | solution.py:264
  33.9 3.8 %all-to-all-done.got_ref = bf16[8,144,128]{2,1,0:T(8,128)(2,1)S(1)} async-done(((bf16[8,144,128]{2,1,0:T(8,128)(2,1)}), bf16[8,144,128]{2,1,0:T(8,128)(2,1)S(1)}, u32[]{:S(2)}, u32[]{:S(2)}) %all-to-all-start) | async-done | bytes 294944 | tf_op jit(solution)/shard_map/all_to_all | solution.py:278
  38.7 11.5 %head_target.1 = (bf16[2,16,2048]{2,1,0:T(8,128)(2,1)S(1)}, bf16[2,16,2048]{2,1,0:T(8,128)(2,1)}, bf16[2,16,2048]{2,1,0:T(8,128)(2,1)S(1)}, bf16[2,16,2048]{2,1,0:T(8,128)(2,1)}, bf16[2048,128]{1,0:T(8,128)(2,1)S(1)}) custom-call(s32[32]{0:T(128)S(1)} %add_multiply_fusion.base_ref, s32[8]{0:T(128)S(1)} %stack.35.offset_ref, ...), custom_call_target="tpu_custom_call" | custom-call | tf_op jit(solution)/shard_map/head_target/pallas_call | solution.py:87
  51.1 2.4 %collective-permute-start.11 = (bf16[2,16,2048]{2,1,0:T(8,128)(2,1)}, bf16[2,16,2048]{2,1,0:T(8,128)(2,1)S(1)}, u32[]{:S(2)}, u32[]{:S(2)}) collective-permute-start(bf16[2,16,2048]{2,1,0:T(8,128)(2,1)} %get-tuple-element.38), channel_id=1, source_target_pairs={{2,0},{4,2},{6,4},{0,6},{3,1},{5,3},{7,5},{1,7},{10,8},{12,10},{14... | collective-permute-start | bytes 393224 | tf_op jit(solution)/shard_map/ppermute | solution.py:264
  55.2 2.8 %collective-permute-done.10 = bf16[2,16,2048]{2,1,0:T(8,128)(2,1)S(1)} collective-permute-done((bf16[2,16,2048]{2,1,0:T(8,128)(2,1)}, bf16[2,16,2048]{2,1,0:T(8,128)(2,1)S(1)}, u32[]{:S(2)}, u32[]{:S(2)}) %collective-permute-start.10) | collective-permute-done | bytes 131104 | tf_op jit(solution)/shard_map/ppermute | solution.py:264
  58.0 2.0 %collective-permute-done.12 = bf16[2,16,2048]{2,1,0:T(8,128)(2,1)S(1)} collective-permute-done((bf16[2,16,2048]{2,1,0:T(8,128)(2,1)S(1)}, bf16[2,16,2048]{2,1,0:T(8,128)(2,1)S(1)}, u32[]{:S(2)}, u32[]{:S(2)}) %collective-permute-start.12) | collective-permute-done | bytes 131104 | tf_op jit(solution)/shard_map/ppermute | solution.py:264
  60.0 3.2 %collective-permute-start.13 = (bf16[16,2048]{1,0:T(8,128)(2,1)S(1)}, bf16[16,2048]{1,0:T(8,128)(2,1)S(1)}, u32[]{:S(2)}, u32[]{:S(2)}) collective-permute-start(bf16[16,2048]{1,0:T(8,128)(2,1)S(1)} %fusion.4), channel_id=1, source_target_pairs={{1,0},{0,1},{3,2},{2,3},{5,4},{4,5},{7,6},{6,7},{9,8},{8,9},{11,10... | collective-permute-start | bytes 196616 | tf_op jit(solution)/shard_map/ppermute | solution.py:264
  63.2 5.3 %collective-permute-done.13.part_ref = bf16[16,2048]{1,0:T(8,128)(2,1)S(1)} collective-permute-done((bf16[16,2048]{1,0:T(8,128)(2,1)S(1)}, bf16[16,2048]{1,0:T(8,128)(2,1)S(1)}, u32[]{:S(2)}, u32[]{:S(2)}) %collective-permute-start.13) | collective-permute-done | bytes 65568 | tf_op jit(solution)/shard_map/ppermute | solution.py:264
  68.5 2.5 %key_backward.1 = f32[32,64,128]{2,1,0:T(8,128)S(1)} custom-call(s32[32]{0:T(128)S(1)} %copy-done.4, bf16[8,144,128]{2,1,0:T(8,128)(2,1)S(1)} %all-to-all-done.got_ref, bf16[2048,128]{1,0:T(8,128)(2,1)S(1)} %get-tuple-element.35.k_ref, f32[16,2048]{1,0:T(8,128)S(1)} %index_prob.1.prob_ref, f32[16,2048]{1,0:T(8,128)S(1)} %slice_bitcast_fusion.near_ref, ...), custom_call_target="tpu_custom_call" | custom-call | tf_op jit(solution)/shard_map/key_backward/pallas_call | solution.py:232
  71.2 1.9 %collective-permute-done.14 = f32[16,64,128]{2,1,0:T(8,128)S(1)} collective-permute-done((f32[16,64,128]{2,1,0:T(8,128)S(1)}, f32[16,64,128]{2,1,0:T(8,128)S(1)}, u32[]{:S(2)}, u32[]{:S(2)}) %collective-permute-start.14) | collective-permute-done | bytes 524320 | tf_op jit(solution)/shard_map/ppermute | solution.py:264
  74.0 2.5 %collective-permute-start.16 = (bf16[4,64,128]{2,1,0:T(8,128)(2,1)S(1)}, bf16[4,64,128]{2,1,0:T(8,128)(2,1)S(1)}, u32[]{:S(2)}, u32[]{:S(2)}) collective-permute-start(bf16[4,64,128]{2,1,0:T(8,128)(2,1)S(1)} %get-tuple-element.57), channel_id=1, source_target_pairs={{64,0},{128,64},{192,128},{0,192},{65,1},{129,65},{193,129},{1,193... | collective-permute-start | bytes 196616 | tf_op jit(solution)/shard_map/ppermute | solution.py:264
  79.0 3.3 %collective-permute-done.17 = bf16[4,64,128]{2,1,0:T(8,128)(2,1)S(1)} collective-permute-done((bf16[4,64,128]{2,1,0:T(8,128)(2,1)S(1)}, bf16[4,64,128]{2,1,0:T(8,128)(2,1)S(1)}, u32[]{:S(2)}, u32[]{:S(2)}) %collective-permute-start.17) | collective-permute-done | bytes 65568 | tf_op jit(solution)/shard_map/ppermute | solution.py:264
  82.3 3.1 %collective-permute-start.18 = (bf16[64,128]{1,0:T(8,128)(2,1)S(1)}, bf16[64,128]{1,0:T(8,128)(2,1)S(1)}, u32[]{:S(2)}, u32[]{:S(2)}) collective-permute-start(bf16[64,128]{1,0:T(8,128)(2,1)S(1)} %get-tuple-element.61), channel_id=1, source_target_pairs={{49,0},{0,16},{16,32},{32,48},{48,1},{1,17},{17,33},{33,49},{51,2}... | collective-permute-start | bytes 49160 | tf_op jit(solution)/shard_map/ppermute | solution.py:269
  85.4 1.7 %collective-permute-start.19 = (bf16[64,128]{1,0:T(8,128)(2,1)S(1)}, bf16[64,128]{1,0:T(8,128)(2,1)S(1)}, u32[]{:S(2)}, u32[]{:S(2)}) collective-permute-start(bf16[64,128]{1,0:T(8,128)(2,1)S(1)} %get-tuple-element.60), channel_id=1, source_target_pairs={{16,0},{32,16},{48,32},{1,48},{17,1},{33,17},{49,33},{0,49},{18,2}... | collective-permute-start | bytes 49160 | tf_op jit(solution)/shard_map/ppermute | solution.py:269
  87.1 1.6 %collective-permute-start.20 = (bf16[64,128]{1,0:T(8,128)(2,1)S(1)}, bf16[64,128]{1,0:T(8,128)(2,1)S(1)}, u32[]{:S(2)}, u32[]{:S(2)}) collective-permute-start(bf16[64,128]{1,0:T(8,128)(2,1)S(1)} %get-tuple-element.59), channel_id=1, source_target_pairs={{32,0},{48,16},{1,32},{17,48},{33,1},{49,17},{0,33},{16,49},{34,2}... | collective-permute-start | bytes 49160 | tf_op jit(solution)/shard_map/ppermute | solution.py:269
  88.7 2.5 %query_backward.1 = bf16[8,144,128]{2,1,0:T(8,128)(2,1)S(1)} custom-call(bf16[8,144,128]{2,1,0:T(8,128)(2,1)S(1)} %all-to-all-done.got_ref, bf16[2048,128]{1,0:T(8,128)(2,1)S(1)} %get-tuple-element.35.k_ref, f32[16,2048]{1,0:T(8,128)S(1)} %index_prob.1.prob_ref, f32[16,2048]{1,0:T(8,128)S(1)} %slice_bitcast_fusion.near_ref, ...), custom_call_target="tpu_custom_call" | custom-call | tf_op jit(solution)/shard_map/query_backward/pallas_call | solution.py:247
  91.3 1.7 %collective-permute-done.20 = bf16[64,128]{1,0:T(8,128)(2,1)S(1)} collective-permute-done((bf16[64,128]{1,0:T(8,128)(2,1)S(1)}, bf16[64,128]{1,0:T(8,128)(2,1)S(1)}, u32[]{:S(2)}, u32[]{:S(2)}) %collective-permute-start.20) | collective-permute-done | bytes 16416 | tf_op jit(solution)/shard_map/ppermute | solution.py:269
  93.0 19.7 %all_to_all.10 = bf16[8,208,128]{2,1,0:T(8,128)(2,1)S(1)} all-to-all(bf16[8,208,128]{2,1,0:T(8,128)(2,1)S(1)} %pad_maximum_fusion), channel_id=1, replica_groups=mesh['y'=4,'z'=4,'c'=2,'x'=4,'w'=2] {'x','w'}, dimensions={0} | all-to-all | bytes 851968 | tf_op jit(solution)/shard_map/all_to_all | solution.py:339
  (69 shorter events, 17.1 us)
Async XLA Ops:
  0.7 32.9 %copy-start.3 = (s32[128]{0:T(128)S(1)}, s32[128]{0:T(128)}, u32[]{:S(2)}) copy-start(s32[128]{0:T(128)} %param.13) | copy-start | bytes 1540
  0.7 37.0 %copy-start = (bf16[128,16,576]{0,2,1:T(8,128)(2,1)S(1)}, bf16[128,16,576]{0,2,1:T(8,128)(2,1)}, u32[]{:S(2)}) copy-start(bf16[128,16,576]{0,2,1:T(8,128)(2,1)} %param.8) | copy-start | bytes 7077892
  1.8 8.7 %collective-permute-start = (bf16[64,768]{1,0:T(8,128)(2,1)S(1)}, bf16[64,768]{1,0:T(8,128)(2,1)S(1)}, u32[]{:S(2)}, u32[]{:S(2)}) collective-permute-start(bf16[64,768]{1,0:T(8,128)(2,1)S(1)} %pad_maximum_fusion.2), channel_id=1, source_target_pairs={{16,0},{32,16},{48,32},{1,48},{17,1},{33,17},{49,33},{0,49},{18,2}... | collective-permute-start | bytes 294920 | tf_op jit(solution)/shard_map/ppermute | solution.py:269
  1.9 8.6 %collective-permute-start.1 = (bf16[64,768]{1,0:T(8,128)(2,1)S(1)}, bf16[64,768]{1,0:T(8,128)(2,1)S(1)}, u32[]{:S(2)}, u32[]{:S(2)}) collective-permute-start(bf16[64,768]{1,0:T(8,128)(2,1)S(1)} %pad_maximum_fusion.2), channel_id=1, source_target_pairs={{49,0},{0,16},{16,32},{32,48},{48,1},{1,17},{17,33},{33,49},{51,2}... | collective-permute-start | bytes 294920 | tf_op jit(solution)/shard_map/ppermute | solution.py:269
  3.9 8.7 %collective-permute-start.2 = (bf16[64,768]{1,0:T(8,128)(2,1)S(1)}, bf16[64,768]{1,0:T(8,128)(2,1)S(1)}, u32[]{:S(2)}, u32[]{:S(2)}) collective-permute-start(bf16[64,768]{1,0:T(8,128)(2,1)S(1)} %pad_maximum_fusion.2), channel_id=1, source_target_pairs={{32,0},{48,16},{1,32},{17,48},{33,1},{49,17},{0,33},{16,49},{34,2}... | collective-permute-start | bytes 294920 | tf_op jit(solution)/shard_map/ppermute | solution.py:269
  13.6 13.8 %collective-permute-start.3 = (bf16[256,768]{1,0:T(8,128)(2,1)S(1)}, bf16[256,768]{1,0:T(8,128)(2,1)}, u32[]{:S(2)}, u32[]{:S(2)}) collective-permute-start(bf16[256,768]{1,0:T(8,128)(2,1)S(1)} %pad_maximum_fusion.1.refs_0_), channel_id=1, source_target_pairs={{128,0},{192,64},{0,128},{64,192},{129,1},{193,65},{1,129},{65,193... | collective-permute-start | bytes 1179656 | tf_op jit(solution)/shard_map/ppermute | solution.py:264
  16.9 16.1 %collective-permute-start.5 = (bf16[256,768]{1,0:T(8,128)(2,1)S(1)}, bf16[256,768]{1,0:T(8,128)(2,1)}, u32[]{:S(2)}, u32[]{:S(2)}) collective-permute-start(bf16[256,768]{1,0:T(8,128)(2,1)S(1)} %pad_maximum_fusion.1.refs_0_), channel_id=1, source_target_pairs={{64,0},{128,64},{192,128},{0,192},{65,1},{129,65},{193,129},{1,193... | collective-permute-start | bytes 1179656 | tf_op jit(solution)/shard_map/ppermute | solution.py:264
  17.9 15.1 %collective-permute-start.6 = (bf16[256,768]{1,0:T(8,128)(2,1)S(1)}, bf16[256,768]{1,0:T(8,128)(2,1)}, u32[]{:S(2)}, u32[]{:S(2)}) collective-permute-start(bf16[256,768]{1,0:T(8,128)(2,1)S(1)} %pad_maximum_fusion.1.refs_0_), channel_id=1, source_target_pairs={{192,0},{0,64},{64,128},{128,192},{193,1},{1,65},{65,129},{129,193... | collective-permute-start | bytes 1179656 | tf_op jit(solution)/shard_map/ppermute | solution.py:264
  18.9 18.8 %all-to-all-start = ((bf16[8,144,128]{2,1,0:T(8,128)(2,1)}), bf16[8,144,128]{2,1,0:T(8,128)(2,1)S(1)}, u32[]{:S(2)}, u32[]{:S(2)}) async-start(bf16[8,144,128]{2,1,0:T(8,128)(2,1)} %pack_index.1), calls=%async_computation | async-start | bytes 589824 | tf_op jit(solution)/shard_map/all_to_all | solution.py:278
  26.3 11.3 %collective-permute-start.7 = (bf16[256,768]{1,0:T(8,128)(2,1)S(1)}, bf16[256,768]{1,0:T(8,128)(2,1)}, u32[]{:S(2)}, u32[]{:S(2)}) collective-permute-start(bf16[256,768]{1,0:T(8,128)(2,1)S(1)} %pad_maximum_fusion.1.refs_0_), channel_id=1, source_target_pairs={{8,0},{0,8},{9,1},{1,9},{10,2},{2,10},{11,3},{3,11},{12,4},{4,12},... | collective-permute-start | bytes 1179656 | tf_op jit(solution)/shard_map/ppermute | solution.py:264
  27.4 10.3 %collective-permute-start.4 = (bf16[256,768]{1,0:T(8,128)(2,1)}, bf16[256,768]{1,0:T(8,128)(2,1)}, u32[]{:S(2)}, u32[]{:S(2)}) collective-permute-start(bf16[256,768]{1,0:T(8,128)(2,1)} %collective-permute-done.3.refs_3_), channel_id=1, source_target_pairs={{8,0},{0,8},{9,1},{1,9},{10,2},{2,10},{11,3},{3,11},{12,4},{4,12},... | collective-permute-start | bytes 1179656 | tf_op jit(solution)/shard_map/ppermute | solution.py:264
  33.0 4.7 %collective-permute-start.8 = (bf16[256,768]{1,0:T(8,128)(2,1)}, bf16[256,768]{1,0:T(8,128)(2,1)}, u32[]{:S(2)}, u32[]{:S(2)}) collective-permute-start(bf16[256,768]{1,0:T(8,128)(2,1)} %collective-permute-done.5.refs_1_), channel_id=1, source_target_pairs={{8,0},{0,8},{9,1},{1,9},{10,2},{2,10},{11,3},{3,11},{12,4},{4,12},... | collective-permute-start | bytes 1179656 | tf_op jit(solution)/shard_map/ppermute | solution.py:264
  33.0 4.7 %collective-permute-start.9 = (bf16[256,768]{1,0:T(8,128)(2,1)}, bf16[256,768]{1,0:T(8,128)(2,1)}, u32[]{:S(2)}, u32[]{:S(2)}) collective-permute-start(bf16[256,768]{1,0:T(8,128)(2,1)} %collective-permute-done.6.refs_2_), channel_id=1, source_target_pairs={{8,0},{0,8},{9,1},{1,9},{10,2},{2,10},{11,3},{3,11},{12,4},{4,12},... | collective-permute-start | bytes 1179656 | tf_op jit(solution)/shard_map/ppermute | solution.py:264
  50.2 7.7 %collective-permute-start.10 = (bf16[2,16,2048]{2,1,0:T(8,128)(2,1)}, bf16[2,16,2048]{2,1,0:T(8,128)(2,1)S(1)}, u32[]{:S(2)}, u32[]{:S(2)}) collective-permute-start(bf16[2,16,2048]{2,1,0:T(8,128)(2,1)} %get-tuple-element.37), channel_id=1, source_target_pairs={{6,0},{0,2},{2,4},{4,6},{7,1},{1,3},{3,5},{5,7},{14,8},{8,10},{10,... | collective-permute-start | bytes 393224 | tf_op jit(solution)/shard_map/ppermute | solution.py:264
  51.1 6.9 %collective-permute-start.11 = (bf16[2,16,2048]{2,1,0:T(8,128)(2,1)}, bf16[2,16,2048]{2,1,0:T(8,128)(2,1)S(1)}, u32[]{:S(2)}, u32[]{:S(2)}) collective-permute-start(bf16[2,16,2048]{2,1,0:T(8,128)(2,1)} %get-tuple-element.38), channel_id=1, source_target_pairs={{2,0},{4,2},{6,4},{0,6},{3,1},{5,3},{7,5},{1,7},{10,8},{12,10},{14... | collective-permute-start | bytes 393224 | tf_op jit(solution)/shard_map/ppermute | solution.py:264
  53.4 6.5 %collective-permute-start.12 = (bf16[2,16,2048]{2,1,0:T(8,128)(2,1)S(1)}, bf16[2,16,2048]{2,1,0:T(8,128)(2,1)S(1)}, u32[]{:S(2)}, u32[]{:S(2)}) collective-permute-start(bf16[2,16,2048]{2,1,0:T(8,128)(2,1)S(1)} %get-tuple-element.39), channel_id=1, source_target_pairs={{4,0},{6,2},{0,4},{2,6},{5,1},{7,3},{1,5},{3,7},{12,8},{14,10},{8,... | collective-permute-start | bytes 393224 | tf_op jit(solution)/shard_map/ppermute | solution.py:264
  60.0 8.5 %collective-permute-start.13 = (bf16[16,2048]{1,0:T(8,128)(2,1)S(1)}, bf16[16,2048]{1,0:T(8,128)(2,1)S(1)}, u32[]{:S(2)}, u32[]{:S(2)}) collective-permute-start(bf16[16,2048]{1,0:T(8,128)(2,1)S(1)} %fusion.4), channel_id=1, source_target_pairs={{1,0},{0,1},{3,2},{2,3},{5,4},{4,5},{7,6},{6,7},{9,8},{8,9},{11,10... | collective-permute-start | bytes 196616 | tf_op jit(solution)/shard_map/ppermute | solution.py:264
  71.1 2.0 %collective-permute-start.14 = (f32[16,64,128]{2,1,0:T(8,128)S(1)}, f32[16,64,128]{2,1,0:T(8,128)S(1)}, u32[]{:S(2)}, u32[]{:S(2)}) collective-permute-start(f32[16,64,128]{2,1,0:T(8,128)S(1)} %slice.64), channel_id=1, source_target_pairs={{8,0},{0,8},{9,1},{1,9},{10,2},{2,10},{11,3},{3,11},{12,4},{4,12},... | collective-permute-start | bytes 1572872 | tf_op jit(solution)/shard_map/ppermute | solution.py:264
  73.2 5.6 %collective-permute-start.15 = (bf16[4,64,128]{2,1,0:T(8,128)(2,1)S(1)}, bf16[4,64,128]{2,1,0:T(8,128)(2,1)S(1)}, u32[]{:S(2)}, u32[]{:S(2)}) collective-permute-start(bf16[4,64,128]{2,1,0:T(8,128)(2,1)S(1)} %get-tuple-element.58), channel_id=1, source_target_pairs={{192,0},{0,64},{64,128},{128,192},{193,1},{1,65},{65,129},{129,193... | collective-permute-start | bytes 196616 | tf_op jit(solution)/shard_map/ppermute | solution.py:264
  74.0 5.0 %collective-permute-start.16 = (bf16[4,64,128]{2,1,0:T(8,128)(2,1)S(1)}, bf16[4,64,128]{2,1,0:T(8,128)(2,1)S(1)}, u32[]{:S(2)}, u32[]{:S(2)}) collective-permute-start(bf16[4,64,128]{2,1,0:T(8,128)(2,1)S(1)} %get-tuple-element.57), channel_id=1, source_target_pairs={{64,0},{128,64},{192,128},{0,192},{65,1},{129,65},{193,129},{1,193... | collective-permute-start | bytes 196616 | tf_op jit(solution)/shard_map/ppermute | solution.py:264
  76.5 5.8 %collective-permute-start.17 = (bf16[4,64,128]{2,1,0:T(8,128)(2,1)S(1)}, bf16[4,64,128]{2,1,0:T(8,128)(2,1)S(1)}, u32[]{:S(2)}, u32[]{:S(2)}) collective-permute-start(bf16[4,64,128]{2,1,0:T(8,128)(2,1)S(1)} %get-tuple-element.56), channel_id=1, source_target_pairs={{128,0},{192,64},{0,128},{64,192},{129,1},{193,65},{1,129},{65,193... | collective-permute-start | bytes 196616 | tf_op jit(solution)/shard_map/ppermute | solution.py:264
  82.3 9.0 %collective-permute-start.18 = (bf16[64,128]{1,0:T(8,128)(2,1)S(1)}, bf16[64,128]{1,0:T(8,128)(2,1)S(1)}, u32[]{:S(2)}, u32[]{:S(2)}) collective-permute-start(bf16[64,128]{1,0:T(8,128)(2,1)S(1)} %get-tuple-element.61), channel_id=1, source_target_pairs={{49,0},{0,16},{16,32},{32,48},{48,1},{1,17},{17,33},{33,49},{51,2}... | collective-permute-start | bytes 49160 | tf_op jit(solution)/shard_map/ppermute | solution.py:269
  85.4 5.9 %collective-permute-start.19 = (bf16[64,128]{1,0:T(8,128)(2,1)S(1)}, bf16[64,128]{1,0:T(8,128)(2,1)S(1)}, u32[]{:S(2)}, u32[]{:S(2)}) collective-permute-start(bf16[64,128]{1,0:T(8,128)(2,1)S(1)} %get-tuple-element.60), channel_id=1, source_target_pairs={{16,0},{32,16},{48,32},{1,48},{17,1},{33,17},{49,33},{0,49},{18,2}... | collective-permute-start | bytes 49160 | tf_op jit(solution)/shard_map/ppermute | solution.py:269
  87.1 5.9 %collective-permute-start.20 = (bf16[64,128]{1,0:T(8,128)(2,1)S(1)}, bf16[64,128]{1,0:T(8,128)(2,1)S(1)}, u32[]{:S(2)}, u32[]{:S(2)}) collective-permute-start(bf16[64,128]{1,0:T(8,128)(2,1)S(1)} %get-tuple-element.59), channel_id=1, source_target_pairs={{32,0},{48,16},{1,32},{17,48},{33,1},{49,17},{0,33},{16,49},{34,2}... | collective-permute-start | bytes 49160 | tf_op jit(solution)/shard_map/ppermute | solution.py:269
  (5 other events, 106.1 us)
